TPU v7x, 256 devices: a whole 4x4x8 slice. The times are simulated.
256 devices in a mesh: row: 8 (over z_lo, x), col: 32 (over z_hi, y, core).
Axes of the slice: x: 4, y: 4, z: 8 (z_hi: 4, z_lo: 2; z = z_hi * 2 + z_lo), core: 2. Of those that a mesh axis runs over, the one named last changes fastest.
Arguments:
- hessian_old: float32 [8192, 24576], P('row', 'col'), may hold values from -6 to 6
- gate_rows: bfloat16 [4096, 8192], P('col', 'row'), may hold values from -9 to 9
- up_rows: bfloat16 [4096, 8192], P('col', 'row'), may hold values from -15 to 15
- gate_columns: bfloat16 [4096, 24576], P('row', 'col'), may hold values from -9 to 9
- up_columns: bfloat16 [4096, 24576], P('row', 'col'), may hold values from -15 to 15
Outputs:
- hessian_new: float32 [8192, 24576], P('row', 'col')
All inputs are finite; a program needn't handle non-finite values.
Results may differ from a plain program's by a relative error of at most 0.00099.
Values may be sent and summed in bfloat16 or wider, within the bound.
No kernel may reach another device: no remote copies, remote signals or barrier semaphores. Data moves between devices by JAX's collectives and lax.ppermute only.
A program may use at most 64 MiB of HBM per device.

v0:
```python
import jax
import jax.numpy as jnp
from jax import lax
from jax.sharding import PartitionSpec as P


def silu_product(gate, up):
    return (jax.nn.silu(gate.astype(jnp.float32)) * up.astype(jnp.float32)).astype(jnp.bfloat16)


def body(hessian_old, gate_rows, up_rows, gate_columns, up_columns):
    total_tokens = lax.axis_size("col") * gate_rows.shape[0]
    row_formed = silu_product(gate_rows, up_rows)
    column_formed = silu_product(gate_columns, up_columns)
    column_gathered = lax.all_gather(column_formed, "row", axis=0, tiled=True)
    product = lax.dot_general(
        lax.all_gather(row_formed, "col", axis=0, tiled=True),
        column_gathered,
        (((0,), (0,)), ((), ())),
        preferred_element_type=jnp.float32,
    )
    return 0.5 * hessian_old + product / total_tokens


def solution(mesh):
    in_specs = (P("row", "col"), P("col", "row"), P("col", "row"), P("row", "col"), P("row", "col"))
    out_specs = P("row", "col")
    return jax.shard_map(body, mesh=mesh, in_specs=in_specs, out_specs=out_specs, check_vma=False)
```

profile of v0, /device:TPU:1, one launch (start us, length us, event | category | flops | bytes accessed | tf_op | source)
XLA Modules:
  0.0 185.5 jit_solution(7823571481103932414)
XLA Ops:
  6.5 0.0 copy-start
  6.5 0.0 copy-start.1
  6.5 0.0 all-gather.5.cloned.1.call-start
  6.5 2.8 %fusion.4 = bf16[512,768]{1,0:T(8,128)(2,1)} fusion(bf16[512,768]{1,0:T(8,128)(2,1)} %param.9, bf16[512,768]{1,0:T(8,128)(2,1)} %param.8), kind=kLoop, calls=%fused_computation.7 | loop fusion | flops 3145728 | bytes 2359296 | tf_op jit(solution)/shard_map/convert_element_type | solution.py:8
  9.3 0.0 all-gather.5.cloned.1.call-update
  9.4 0.0 all-gather.3.cloned.1.call-start
  9.4 0.0 copy-done
  9.4 0.0 copy-done.1
  9.4 0.9 fusion.9
  10.3 0.0 all-gather.3.cloned.1.call-update
  10.3 77.8 %all-gather.5.cloned.1.call-done = bf16[4096,768]{1,0:T(8,128)(2,1)} async-done(((bf16[512,768]{1,0:T(8,128)(2,1)}), bf16[4096,768]{1,0:T(8,128)(2,1)}) %all-gather.5.cloned.1.call-update) | async-done | bytes 6291472 | tf_op jit(solution)/shard_map/all_gather | solution.py:15
  88.2 77.9 %all-gather.3.cloned.1.call-done = bf16[4096,1024]{1,0:T(8,128)(2,1)} async-done(((bf16[128,1024]{1,0:T(8,128)(2,1)}), bf16[4096,1024]{1,0:T(8,128)(2,1)}) %all-gather.3.cloned.1.call-update) | async-done | bytes 8388624 | tf_op jit(solution)/shard_map/all_gather | solution.py:17
  166.0 12.6 %multiply_add_fusion = f32[1024,768]{1,0:T(8,128)} fusion(f32[1024,768]{1,0:T(8,128)} %param.5, bf16[4096,1024]{1,0:T(8,128)(2,1)} %all-gather.3.cloned.1.call-done, bf16[4096,768]{1,0:T(8,128)(2,1)} %all-gather.5.cloned.1.call-done), kind=kOutput, calls=%fused_computation | convolution fusion | flops 6444810240 | bytes 20971520 | tf_op jit(solution)/shard_map/dot_general | solution.py:16
Async XLA Ops:
  6.5 2.9 %copy-start = (bf16[128,1024]{1,0:T(8,128)(2,1)S(1)}, bf16[128,1024]{1,0:T(8,128)(2,1)}, u32[]{:S(2)}) copy-start(bf16[128,1024]{1,0:T(8,128)(2,1)} %param.7) | copy-start | bytes 786436
  6.5 2.9 %copy-start.1 = (bf16[128,1024]{1,0:T(8,128)(2,1)S(1)}, bf16[128,1024]{1,0:T(8,128)(2,1)}, u32[]{:S(2)}) copy-start(bf16[128,1024]{1,0:T(8,128)(2,1)} %param.6) | copy-start | bytes 786436
  6.5 81.6 %all-gather.5.cloned.1.call-start = ((), (), s32[]{:S(2)}) async-start(), calls=%async_computation.1 | async-start | bytes 7077888 | tf_op jit(solution)/shard_map/all_gather | solution.py:15
  9.4 156.7 %all-gather.3.cloned.1.call-start = ((), (), s32[]{:S(2)}) async-start(), calls=%async_computation | async-start | bytes 8650752 | tf_op jit(solution)/shard_map/all_gather | solution.py:17
Sparse Core Ops, SparseCore 0:
  9.5 78.6 all-gather.4
  90.7 75.2 all-gather.2
where the time goes:
time: 187 us; the launch traced here: 185 us
  waiting for transfers between devices  156 us (83%)
  between operations  13.4 us (7%)
  matrix products  12.6 us (7%)
  other arithmetic  3.68 us (2%)
    all_gather x1, waiting for transfers between devices, body(): lax.all_gather(row_formed, 'col', axis=0, tiled=True)  77.9 us
    all_gather x1, waiting for transfers between devices, body(): column_gathered = lax.all_gather(column_formed, 'row', axis=0, tiled=True)  77.8 us
    dot_general x1, matrix products, body(): lax.dot_general(lax.all_gather(row_formed, 'col', axis=0, tiled=True), co...  12.6 us
  transfers between devices with their start and end apart: 2, of which 2 were waited for; matrix products, arithmetic and copies ran while one was open for 0% of the time, Pallas kernels for 0%

commit v1 on v0

v1 whole, which is shorter than its diff:
```python
import jax
import jax.numpy as jnp
from jax import lax
from jax.sharding import PartitionSpec as P

AXES = ("row", "col")


def place(x, y, z, c):
    x, y, z = x % 4, y % 4, z % 8
    return ((z % 2) * 4 + x) * 32 + ((z // 2) * 4 + y) * 2 + c


def send(value, dx=0, dy=0, dz=0, swap_z=False, swap_core=False):
    pairs = []
    for x in range(4):
        for y in range(4):
            for z in range(8):
                for c in range(2):
                    to_z = (z ^ 1) if swap_z else z + dz
                    pairs.append((place(x, y, z, c), place(x + dx, y + dy, to_z, c ^ int(swap_core))))
    return lax.ppermute(value, AXES, pairs)


def silu_product(gate, up):
    return (jax.nn.silu(gate.astype(jnp.float32)) * up.astype(jnp.float32)).astype(jnp.bfloat16)


def body(hessian_old, gate_rows, up_rows, gate_columns, up_columns):
    total_tokens = lax.axis_size("col") * gate_rows.shape[0]
    row, col = lax.axis_index("row"), lax.axis_index("col")
    zl, x = row // 4, row % 4
    zh, y, c = col // 8, (col // 2) % 4, col % 2

    own = silu_product(gate_columns, up_columns)
    own_rows = silu_product(gate_rows, up_rows)

    pair = send(own, swap_z=True)
    columns = {(0, 0): own, (1, 0): pair}
    columns[0, 2] = send(own, dx=2)
    z_rows = {0: own_rows, 2: send(own_rows, dz=4), 1: send(own_rows, dz=2), 3: send(own_rows, dz=-2)}
    columns[0, 1] = send(own, dx=1)
    columns[0, 3] = send(own, dx=-1)
    columns[1, 2] = send(pair, dx=2)
    columns[1, 1] = send(pair, dx=1)
    columns[1, 3] = send(pair, dx=-1)

    z_block = jnp.zeros((4,) + own_rows.shape, own_rows.dtype)
    for back, block in z_rows.items():
        z_block = lax.dynamic_update_slice(z_block, block[None], ((zh - back) % 4, 0, 0))
    y_blocks = {0: z_block, 2: send(z_block, dy=2), 1: send(z_block, dy=1), 3: send(z_block, dy=-1)}
    rows = jnp.zeros((4, 4, 2) + own_rows.shape, own_rows.dtype)
    for back, block in y_blocks.items():
        rows = lax.dynamic_update_slice(rows, block[:, None, None], (0, (y - back) % 4, c, 0, 0))
        other = send(block, swap_core=True)
        rows = lax.dynamic_update_slice(rows, other[:, None, None], (0, (y - back) % 4, 1 - c, 0, 0))
    rows = rows.reshape(4096, -1)

    total = 0.5 * hessian_old
    for (back_z, back_x), block in columns.items():
        shard = ((zl + back_z) % 2) * 4 + (x - back_x) % 4
        part = lax.dynamic_slice(rows, (shard * 512, 0), (512, rows.shape[1]))
        product = lax.dot_general(part, block, (((0,), (0,)), ((), ())), preferred_element_type=jnp.float32)
        total = total + product / total_tokens
    return total


def solution(mesh):
    in_specs = (P("row", "col"), P("col", "row"), P("col", "row"), P("row", "col"), P("row", "col"))
    out_specs = P("row", "col")
    return jax.shard_map(body, mesh=mesh, in_specs=in_specs, out_specs=out_specs, check_vma=False)
```

time: 187 us -> 175 us (0.936)
  waiting for transfers between devices: 156 us -> 114 us
  starting transfers between devices: 0.04 us -> 30.2 us
  between operations: 13.4 us -> 0.18 us
  matrix products: 12.6 us -> 20.7 us
  local copies, waits for them, and re-layouts: 0.01 us -> 5.77 us
    all_gather x2 -> x0, waiting for transfers between devices: 156 us -> none  [the longest x1 77.9 us: body(): lax.all_gather(row_formed, 'col', axis=0, tiled=True)]
    ppermute x0 -> x17, waiting for transfers between devices: none -> 114 us  [send(): return lax.ppermute(value, AXES, pairs)]
    ppermute x0 -> x17, starting transfers between devices: none -> 30.2 us  [send(): return lax.ppermute(value, AXES, pairs)]
    dot_general x1 -> x8, matrix products: 12.6 us -> 20.7 us  [body(): lax.dot_general(part, block, (((0,), (0,)), ((), ())), preferred_element_...]
    dynamic_update_slice x0 -> x11, local copies, waits for them, and re-layouts: none -> 4.59 us  [the longest x4 2.86 us: body(): lax.dynamic_update_slice(rows, other[:, None, None], (0, (y - back) % 4,...]
  transfers between devices with their start and end apart: 2 -> 17, of which waited for: 2 -> 8; matrix products, arithmetic and copies ran while one was open for 0% -> 13% of each run, Pallas kernels for 0% -> 0%
where the time goes in v1:
time: 175 us; the launch traced here: 174 us
  waiting for transfers between devices  114 us (65%)
  starting transfers between devices  30.2 us (17%)
  matrix products  20.7 us (12%)
  local copies, waits for them, and re-layouts  5.77 us (3%)
  other arithmetic  3.96 us (2%)
    ppermute x17, waiting for transfers between devices, send(): return lax.ppermute(value, AXES, pairs)  114 us
    ppermute x17, starting transfers between devices, send(): return lax.ppermute(value, AXES, pairs)  30.2 us
    dot_general x8, matrix products, body(): lax.dot_general(part, block, (((0,), (0,)), ((), ())), preferred_element_...  20.7 us
  transfers between devices with their start and end apart: 17, of which 8 were waited for; matrix products, arithmetic and copies ran while one was open for 13% of the time, Pallas kernels for 0%

profile of v1, /device:TPU:1, one launch (start us, length us, event | category | flops | bytes accessed | tf_op | source)
XLA Modules:
  0.0 174.4 jit_solution(14693891096283950483)
XLA Ops:
  0.0 0.1 broadcast_in_dim.43
  0.1 1.2 bitcast_dynamic-update-slice_fusion.11
  1.3 7.8 %collective-permute-start = (bf16[128,1024]{1,0:T(8,128)(2,1)S(1)}, bf16[128,1024]{1,0:T(8,128)(2,1)S(1)}, u32[]{:S(2)}, u32[]{:S(2)}) collective-permute-start(bf16[128,1024]{1,0:T(8,128)(2,1)S(1)} %get-tuple-element.6), channel_id=1, source_target_pairs={{0,16},{1,17},{128,144},{129,145},{8,24},{9,25},{136,152},{137,153... | collective-permute-start | bytes 786440 | tf_op jit(solution)/shard_map/ppermute | solution.py:22
  9.2 1.2 collective-permute-start.1
  10.4 2.4 %collective-permute-start.2 = (bf16[128,1024]{1,0:T(8,128)(2,1)S(1)}, bf16[128,1024]{1,0:T(8,128)(2,1)S(1)}, u32[]{:S(2)}, u32[]{:S(2)}) collective-permute-start(bf16[128,1024]{1,0:T(8,128)(2,1)S(1)} %get-tuple-element.6), channel_id=1, source_target_pairs={{0,24},{1,25},{128,152},{129,153},{8,0},{9,1},{136,128},{137,129},... | collective-permute-start | bytes 786440 | tf_op jit(solution)/shard_map/ppermute | solution.py:22
  12.7 3.5 %collective-permute-done = bf16[128,1024]{1,0:T(8,128)(2,1)S(1)} collective-permute-done((bf16[128,1024]{1,0:T(8,128)(2,1)S(1)}, bf16[128,1024]{1,0:T(8,128)(2,1)S(1)}, u32[]{:S(2)}, u32[]{:S(2)}) %collective-permute-start) | collective-permute-done | bytes 262176 | tf_op jit(solution)/shard_map/ppermute | solution.py:22
  16.3 11.2 %collective-permute-done.1 = bf16[128,1024]{1,0:T(8,128)(2,1)S(1)} collective-permute-done((bf16[128,1024]{1,0:T(8,128)(2,1)S(1)}, bf16[128,1024]{1,0:T(8,128)(2,1)S(1)}, u32[]{:S(2)}, u32[]{:S(2)}) %collective-permute-start.1) | collective-permute-done | bytes 262176 | tf_op jit(solution)/shard_map/ppermute | solution.py:22
  27.5 5.9 %collective-permute-done.2 = bf16[128,1024]{1,0:T(8,128)(2,1)S(1)} collective-permute-done((bf16[128,1024]{1,0:T(8,128)(2,1)S(1)}, bf16[128,1024]{1,0:T(8,128)(2,1)S(1)}, u32[]{:S(2)}, u32[]{:S(2)}) %collective-permute-start.2) | collective-permute-done | bytes 262176 | tf_op jit(solution)/shard_map/ppermute | solution.py:22
  33.4 3.0 %collective-permute-start.4 = (bf16[4,128,1024]{2,1,0:T(8,128)(2,1)S(1)}, bf16[4,128,1024]{2,1,0:T(8,128)(2,1)}, u32[]{:S(2)}, u32[]{:S(2)}) collective-permute-start(bf16[4,128,1024]{2,1,0:T(8,128)(2,1)S(1)} %bitcast_dynamic-update-slice_fusion.8), channel_id=1, source_target_pairs={{0,4},{1,5},{128,132},{129,133},{8,12},{9,13},{136,140},{137,141},... | collective-permute-start | bytes 3145736 | tf_op jit(solution)/shard_map/ppermute | solution.py:22
  36.4 0.4 collective-permute-start.6
  36.8 1.1 collective-permute-start.3
  37.9 2.3 %collective-permute-start.8 = (bf16[4,128,1024]{2,1,0:T(8,128)(2,1)S(1)}, bf16[4,128,1024]{2,1,0:T(8,128)(2,1)S(1)}, u32[]{:S(2)}, u32[]{:S(2)}) collective-permute-start(bf16[4,128,1024]{2,1,0:T(8,128)(2,1)S(1)} %bitcast_dynamic-update-slice_fusion.8), channel_id=1, source_target_pairs={{0,6},{1,7},{128,134},{129,135},{8,14},{9,15},{136,142},{137,143},... | collective-permute-start | bytes 3145736 | tf_op jit(solution)/shard_map/ppermute | solution.py:22
  40.2 19.1 %collective-permute-done.4 = bf16[4,128,1024]{2,1,0:T(8,128)(2,1)} collective-permute-done((bf16[4,128,1024]{2,1,0:T(8,128)(2,1)S(1)}, bf16[4,128,1024]{2,1,0:T(8,128)(2,1)}, u32[]{:S(2)}, u32[]{:S(2)}) %collective-permute-start.4) | collective-permute-done | bytes 1048608 | tf_op jit(solution)/shard_map/ppermute | solution.py:22
  59.3 2.4 %collective-permute-start.5 = (bf16[4,128,1024]{2,1,0:T(8,128)(2,1)}, bf16[4,128,1024]{2,1,0:T(8,128)(2,1)}, u32[]{:S(2)}, u32[]{:S(2)}) collective-permute-start(bf16[4,128,1024]{2,1,0:T(8,128)(2,1)} %collective-permute-done.4), channel_id=1, source_target_pairs={{0,1},{1,0},{128,129},{129,128},{8,9},{9,8},{136,137},{137,136},{1... | collective-permute-start | bytes 3145736 | tf_op jit(solution)/shard_map/ppermute | solution.py:22
  61.7 2.7 %fusion.4 = bf16[512,768]{1,0:T(8,128)(2,1)} fusion(bf16[512,768]{1,0:T(8,128)(2,1)} %param.9, bf16[512,768]{1,0:T(8,128)(2,1)} %param.8), kind=kLoop, calls=%fused_computation.7 | loop fusion | flops 3145728 | bytes 2359296 | tf_op jit(solution)/shard_map/convert_element_type | solution.py:26
  64.5 2.5 %collective-permute-start.13 = (bf16[512,768]{1,0:T(8,128)(2,1)}, bf16[512,768]{1,0:T(8,128)(2,1)}, u32[]{:S(2)}, u32[]{:S(2)}) collective-permute-start(bf16[512,768]{1,0:T(8,128)(2,1)} %fusion.4), channel_id=1, source_target_pairs={{0,96},{1,97},{128,224},{129,225},{8,104},{9,105},{136,232},{137,2... | collective-permute-start | bytes 2359304 | tf_op jit(solution)/shard_map/ppermute | solution.py:22
  67.0 1.1 broadcast_in_dim.42
  68.0 0.1 bitcast_dynamic-update-slice_fusion.6
  68.1 14.4 %collective-permute-done.6 = bf16[4,128,1024]{2,1,0:T(8,128)(2,1)S(1)} collective-permute-done((bf16[4,128,1024]{2,1,0:T(8,128)(2,1)S(1)}, bf16[4,128,1024]{2,1,0:T(8,128)(2,1)S(1)}, u32[]{:S(2)}, u32[]{:S(2)}) %collective-permute-start.6) | collective-permute-done | bytes 1048608 | tf_op jit(solution)/shard_map/ppermute | solution.py:22
  82.6 0.0 collective-permute-start.10
  82.6 0.0 collective-permute-done.3
  82.6 0.5 collective-permute-start.7
  83.1 1.3 bitcast_dynamic-update-slice_fusion.5
  84.4 1.3 bitcast_dynamic-update-slice_fusion.4
  85.7 0.0 collective-permute-done.8
  85.7 1.3 collective-permute-start.12
  87.1 0.0 collective-permute-done.5
  87.1 0.3 collective-permute-start.9
  87.3 1.3 bitcast_dynamic-update-slice_fusion.3
  88.7 0.1 bitcast_dynamic-update-slice_fusion.2
  88.8 12.6 %collective-permute-done.10 = bf16[512,768]{1,0:T(8,128)(2,1)S(1)} collective-permute-done((bf16[512,768]{1,0:T(8,128)(2,1)}, bf16[512,768]{1,0:T(8,128)(2,1)S(1)}, u32[]{:S(2)}, u32[]{:S(2)}) %collective-permute-start.10) | collective-permute-done | bytes 786464 | tf_op jit(solution)/shard_map/ppermute | solution.py:22
  101.4 2.7 %collective-permute-start.11 = (bf16[512,768]{1,0:T(8,128)(2,1)}, bf16[512,768]{1,0:T(8,128)(2,1)S(1)}, u32[]{:S(2)}, u32[]{:S(2)}) collective-permute-start(bf16[512,768]{1,0:T(8,128)(2,1)} %fusion.4), channel_id=1, source_target_pairs={{0,64},{1,65},{128,192},{129,193},{8,72},{9,73},{136,200},{137,201... | collective-permute-start | bytes 2359304 | tf_op jit(solution)/shard_map/ppermute | solution.py:22
  104.1 0.0 collective-permute-done.7
  104.1 0.5 collective-permute-start.15
  104.7 0.1 bitcast_dynamic-update-slice_fusion.1
  104.8 0.1 bitcast_dynamic-update-slice_fusion
  104.9 0.0 collective-permute-done.9
  104.9 1.6 collective-permute-start.14
  106.5 0.1 bitcast_dynamic-update-slice_fusion.7
  106.6 2.2 %fusion.18 = f32[1024,768]{1,0:T(8,128)S(1)} fusion(bf16[512,768]{1,0:T(8,128)(2,1)} %fusion.4, bf16[4096,1024]{1,0:T(8,128)(2,1)S(1)} %bitcast.47, s32[]{:T(128)S(6)} %select_n.199), kind=kOutput, calls=%fused_computation.29 | convolution fusion | flops 805306368 | bytes 4980740 | tf_op jit(solution)/shard_map/dot_general | solution.py:63
  108.8 1.0 fusion.16
  109.8 31.4 %collective-permute-done.15 = bf16[512,768]{1,0:T(8,128)(2,1)S(1)} collective-permute-done((bf16[512,768]{1,0:T(8,128)(2,1)S(1)}, bf16[512,768]{1,0:T(8,128)(2,1)S(1)}, u32[]{:S(2)}, u32[]{:S(2)}) %collective-permute-start.15) | collective-permute-done | bytes 786464 | tf_op jit(solution)/shard_map/ppermute | solution.py:22
  141.2 0.1 collective-permute-start.16
  141.4 1.0 fusion.6
  142.4 15.5 %collective-permute-done.14 = bf16[512,768]{1,0:T(8,128)(2,1)S(1)} collective-permute-done((bf16[512,768]{1,0:T(8,128)(2,1)S(1)}, bf16[512,768]{1,0:T(8,128)(2,1)S(1)}, u32[]{:S(2)}, u32[]{:S(2)}) %collective-permute-start.14) | collective-permute-done | bytes 786464 | tf_op jit(solution)/shard_map/ppermute | solution.py:22
  158.0 1.0 fusion.8
  159.0 0.0 collective-permute-done.13
  159.0 3.8 %fusion.10 = f32[1024,768]{1,0:T(8,128)} fusion(bf16[512,768]{1,0:T(8,128)(2,1)} %collective-permute-done.13, bf16[4096,1024]{1,0:T(8,128)(2,1)S(1)} %bitcast.51, s32[]{:T(128)S(6)} %select_n.207), kind=kOutput, calls=%fused_computation.21 | convolution fusion | flops 805306368 | bytes 4980740 | tf_op jit(solution)/shard_map/dot_general | solution.py:63
  162.8 0.0 collective-permute-done.12
  162.8 2.7 %fusion.12 = f32[1024,768]{1,0:T(8,128)} fusion(bf16[512,768]{1,0:T(8,128)(2,1)S(1)} %collective-permute-done.12, bf16[4096,1024]{1,0:T(8,128)(2,1)S(1)} %bitcast.52, s32[]{:T(128)S(6)} %select_n.205), kind=kOutput, calls=%fused_computation.23 | convolution fusion | flops 805306368 | bytes 4980740 | tf_op jit(solution)/shard_map/dot_general | solution.py:63
  165.5 0.0 copy-start
  165.5 0.0 collective-permute-done.11
  165.5 2.7 %fusion.14 = f32[1024,768]{1,0:T(8,128)} fusion(bf16[512,768]{1,0:T(8,128)(2,1)S(1)} %collective-permute-done.11, bf16[4096,1024]{1,0:T(8,128)(2,1)S(1)} %bitcast.53, s32[]{:T(128)S(6)} %select_n.203), kind=kOutput, calls=%fused_computation.25 | convolution fusion | flops 805306368 | bytes 4980740 | tf_op jit(solution)/shard_map/dot_general | solution.py:63
  168.2 0.0 collective-permute-done.16
  168.2 0.0 copy-done
  168.2 6.2 %multiply_add_fusion = f32[1024,768]{1,0:T(8,128)} fusion(f32[1024,768]{1,0:T(8,128)S(1)} %fusion.6, f32[1024,768]{1,0:T(8,128)S(1)} %fusion.8, f32[1024,768]{1,0:T(8,128)} %fusion.10, f32[1024,768]{1,0:T(8,128)} %fusion.12, f32[1024,768]{1,0:T(8,128)} %fusion.14, f32[1024,768]{1,0:T(8,128)S(1)} %fusion.16, f32[1024,768]{1,0:T(8,128)S(1)} %fusion.18, ...), kind=kOutput, calls=%fused_computation | convolution fusion | flops 818675712 | bytes 30146564 | tf_op jit(solution)/shard_map/dot_general | solution.py:63
  (3 shorter events, 0.1 us)
Async XLA Ops:
  1.3 14.9 %collective-permute-start = (bf16[128,1024]{1,0:T(8,128)(2,1)S(1)}, bf16[128,1024]{1,0:T(8,128)(2,1)S(1)}, u32[]{:S(2)}, u32[]{:S(2)}) collective-permute-start(bf16[128,1024]{1,0:T(8,128)(2,1)S(1)} %get-tuple-element.6), channel_id=1, source_target_pairs={{0,16},{1,17},{128,144},{129,145},{8,24},{9,25},{136,152},{137,153... | collective-permute-start | bytes 786440 | tf_op jit(solution)/shard_map/ppermute | solution.py:22
  9.2 18.3 %collective-permute-start.1 = (bf16[128,1024]{1,0:T(8,128)(2,1)S(1)}, bf16[128,1024]{1,0:T(8,128)(2,1)S(1)}, u32[]{:S(2)}, u32[]{:S(2)}) collective-permute-start(bf16[128,1024]{1,0:T(8,128)(2,1)S(1)} %get-tuple-element.6), channel_id=1, source_target_pairs={{0,8},{1,9},{128,136},{129,137},{8,16},{9,17},{136,144},{137,145},... | collective-permute-start | bytes 786440 | tf_op jit(solution)/shard_map/ppermute | solution.py:22
  10.4 23.0 %collective-permute-start.2 = (bf16[128,1024]{1,0:T(8,128)(2,1)S(1)}, bf16[128,1024]{1,0:T(8,128)(2,1)S(1)}, u32[]{:S(2)}, u32[]{:S(2)}) collective-permute-start(bf16[128,1024]{1,0:T(8,128)(2,1)S(1)} %get-tuple-element.6), channel_id=1, source_target_pairs={{0,24},{1,25},{128,152},{129,153},{8,0},{9,1},{136,128},{137,129},... | collective-permute-start | bytes 786440 | tf_op jit(solution)/shard_map/ppermute | solution.py:22
  33.4 25.9 %collective-permute-start.4 = (bf16[4,128,1024]{2,1,0:T(8,128)(2,1)S(1)}, bf16[4,128,1024]{2,1,0:T(8,128)(2,1)}, u32[]{:S(2)}, u32[]{:S(2)}) collective-permute-start(bf16[4,128,1024]{2,1,0:T(8,128)(2,1)S(1)} %bitcast_dynamic-update-slice_fusion.8), channel_id=1, source_target_pairs={{0,4},{1,5},{128,132},{129,133},{8,12},{9,13},{136,140},{137,141},... | collective-permute-start | bytes 3145736 | tf_op jit(solution)/shard_map/ppermute | solution.py:22
  36.4 46.1 %collective-permute-start.6 = (bf16[4,128,1024]{2,1,0:T(8,128)(2,1)S(1)}, bf16[4,128,1024]{2,1,0:T(8,128)(2,1)S(1)}, u32[]{:S(2)}, u32[]{:S(2)}) collective-permute-start(bf16[4,128,1024]{2,1,0:T(8,128)(2,1)S(1)} %bitcast_dynamic-update-slice_fusion.8), channel_id=1, source_target_pairs={{0,2},{1,3},{128,130},{129,131},{8,10},{9,11},{136,138},{137,139},... | collective-permute-start | bytes 3145736 | tf_op jit(solution)/shard_map/ppermute | solution.py:22
  36.8 45.7 %collective-permute-start.3 = (bf16[4,128,1024]{2,1,0:T(8,128)(2,1)S(1)}, bf16[4,128,1024]{2,1,0:T(8,128)(2,1)}, u32[]{:S(2)}, u32[]{:S(2)}) collective-permute-start(bf16[4,128,1024]{2,1,0:T(8,128)(2,1)S(1)} %bitcast_dynamic-update-slice_fusion.8), channel_id=1, source_target_pairs={{0,1},{1,0},{128,129},{129,128},{8,9},{9,8},{136,137},{137,136},{1... | collective-permute-start | bytes 3145736 | tf_op jit(solution)/shard_map/ppermute | solution.py:22
  37.9 47.8 %collective-permute-start.8 = (bf16[4,128,1024]{2,1,0:T(8,128)(2,1)S(1)}, bf16[4,128,1024]{2,1,0:T(8,128)(2,1)S(1)}, u32[]{:S(2)}, u32[]{:S(2)}) collective-permute-start(bf16[4,128,1024]{2,1,0:T(8,128)(2,1)S(1)} %bitcast_dynamic-update-slice_fusion.8), channel_id=1, source_target_pairs={{0,6},{1,7},{128,134},{129,135},{8,14},{9,15},{136,142},{137,143},... | collective-permute-start | bytes 3145736 | tf_op jit(solution)/shard_map/ppermute | solution.py:22
  59.3 27.7 %collective-permute-start.5 = (bf16[4,128,1024]{2,1,0:T(8,128)(2,1)}, bf16[4,128,1024]{2,1,0:T(8,128)(2,1)}, u32[]{:S(2)}, u32[]{:S(2)}) collective-permute-start(bf16[4,128,1024]{2,1,0:T(8,128)(2,1)} %collective-permute-done.4), channel_id=1, source_target_pairs={{0,1},{1,0},{128,129},{129,128},{8,9},{9,8},{136,137},{137,136},{1... | collective-permute-start | bytes 3145736 | tf_op jit(solution)/shard_map/ppermute | solution.py:22
  64.5 94.5 %collective-permute-start.13 = (bf16[512,768]{1,0:T(8,128)(2,1)}, bf16[512,768]{1,0:T(8,128)(2,1)}, u32[]{:S(2)}, u32[]{:S(2)}) collective-permute-start(bf16[512,768]{1,0:T(8,128)(2,1)} %fusion.4), channel_id=1, source_target_pairs={{0,96},{1,97},{128,224},{129,225},{8,104},{9,105},{136,232},{137,2... | collective-permute-start | bytes 2359304 | tf_op jit(solution)/shard_map/ppermute | solution.py:22
  82.6 18.8 %collective-permute-start.10 = (bf16[512,768]{1,0:T(8,128)(2,1)}, bf16[512,768]{1,0:T(8,128)(2,1)S(1)}, u32[]{:S(2)}, u32[]{:S(2)}) collective-permute-start(bf16[512,768]{1,0:T(8,128)(2,1)} %fusion.4), channel_id=1, source_target_pairs={{0,128},{1,129},{128,0},{129,1},{8,136},{9,137},{136,8},{137,9},{1... | collective-permute-start | bytes 2359304 | tf_op jit(solution)/shard_map/ppermute | solution.py:22
  82.6 21.6 %collective-permute-start.7 = (bf16[4,128,1024]{2,1,0:T(8,128)(2,1)S(1)}, bf16[4,128,1024]{2,1,0:T(8,128)(2,1)S(1)}, u32[]{:S(2)}, u32[]{:S(2)}) collective-permute-start(bf16[4,128,1024]{2,1,0:T(8,128)(2,1)S(1)} %collective-permute-done.6), channel_id=1, source_target_pairs={{0,1},{1,0},{128,129},{129,128},{8,9},{9,8},{136,137},{137,136},{1... | collective-permute-start | bytes 3145736 | tf_op jit(solution)/shard_map/ppermute | solution.py:22
  85.7 77.1 %collective-permute-start.12 = (bf16[512,768]{1,0:T(8,128)(2,1)}, bf16[512,768]{1,0:T(8,128)(2,1)S(1)}, u32[]{:S(2)}, u32[]{:S(2)}) collective-permute-start(bf16[512,768]{1,0:T(8,128)(2,1)} %fusion.4), channel_id=1, source_target_pairs={{0,32},{1,33},{128,160},{129,161},{8,40},{9,41},{136,168},{137,169... | collective-permute-start | bytes 2359304 | tf_op jit(solution)/shard_map/ppermute | solution.py:22
  87.1 17.8 %collective-permute-start.9 = (bf16[4,128,1024]{2,1,0:T(8,128)(2,1)S(1)}, bf16[4,128,1024]{2,1,0:T(8,128)(2,1)S(1)}, u32[]{:S(2)}, u32[]{:S(2)}) collective-permute-start(bf16[4,128,1024]{2,1,0:T(8,128)(2,1)S(1)} %collective-permute-done.8), channel_id=1, source_target_pairs={{0,1},{1,0},{128,129},{129,128},{8,9},{9,8},{136,137},{137,136},{1... | collective-permute-start | bytes 3145736 | tf_op jit(solution)/shard_map/ppermute | solution.py:22
  101.4 64.1 %collective-permute-start.11 = (bf16[512,768]{1,0:T(8,128)(2,1)}, bf16[512,768]{1,0:T(8,128)(2,1)S(1)}, u32[]{:S(2)}, u32[]{:S(2)}) collective-permute-start(bf16[512,768]{1,0:T(8,128)(2,1)} %fusion.4), channel_id=1, source_target_pairs={{0,64},{1,65},{128,192},{129,193},{8,72},{9,73},{136,200},{137,201... | collective-permute-start | bytes 2359304 | tf_op jit(solution)/shard_map/ppermute | solution.py:22
  104.1 37.1 %collective-permute-start.15 = (bf16[512,768]{1,0:T(8,128)(2,1)S(1)}, bf16[512,768]{1,0:T(8,128)(2,1)S(1)}, u32[]{:S(2)}, u32[]{:S(2)}) collective-permute-start(bf16[512,768]{1,0:T(8,128)(2,1)S(1)} %collective-permute-done.10), channel_id=1, source_target_pairs={{0,32},{1,33},{128,160},{129,161},{8,40},{9,41},{136,168},{137,169... | collective-permute-start | bytes 2359304 | tf_op jit(solution)/shard_map/ppermute | solution.py:22
  104.9 53.1 %collective-permute-start.14 = (bf16[512,768]{1,0:T(8,128)(2,1)S(1)}, bf16[512,768]{1,0:T(8,128)(2,1)S(1)}, u32[]{:S(2)}, u32[]{:S(2)}) collective-permute-start(bf16[512,768]{1,0:T(8,128)(2,1)S(1)} %collective-permute-done.10), channel_id=1, source_target_pairs={{0,64},{1,65},{128,192},{129,193},{8,72},{9,73},{136,200},{137,201... | collective-permute-start | bytes 2359304 | tf_op jit(solution)/shard_map/ppermute | solution.py:22
  141.2 27.0 %collective-permute-start.16 = (bf16[512,768]{1,0:T(8,128)(2,1)S(1)}, bf16[512,768]{1,0:T(8,128)(2,1)S(1)}, u32[]{:S(2)}, u32[]{:S(2)}) collective-permute-start(bf16[512,768]{1,0:T(8,128)(2,1)S(1)} %collective-permute-done.10), channel_id=1, source_target_pairs={{0,96},{1,97},{128,224},{129,225},{8,104},{9,105},{136,232},{137,2... | collective-permute-start | bytes 2359304 | tf_op jit(solution)/shard_map/ppermute | solution.py:22
  165.5 2.7 %copy-start = (f32[1024,768]{1,0:T(8,128)S(1)}, f32[1024,768]{1,0:T(8,128)}, u32[]{:S(2)}) copy-start(f32[1024,768]{1,0:T(8,128)} %param.5) | copy-start | bytes 9437188

commit v2 on v0

v2 whole, which is shorter than its diff:
```python
import functools

import jax
import jax.numpy as jnp
from jax import lax
from jax.experimental import pallas as pl
from jax.experimental.pallas import tpu as pltpu
from jax.sharding import PartitionSpec as P

AXES = ("row", "col")
CHUNK = 512
VMEM = pl.BlockSpec(memory_space=pltpu.VMEM)
SMEM = pl.BlockSpec(memory_space=pltpu.SMEM)
HBM = pl.BlockSpec(memory_space=pltpu.HBM)


def place(x, y, z, c):
    x, y, z = x % 4, y % 4, z % 8
    return ((z % 2) * 4 + x) * 32 + ((z // 2) * 4 + y) * 2 + c


def send(value, target, after=()):
    if after:
        value = lax.optimization_barrier((value, *after))[0]
    pairs = []
    for x in range(4):
        for y in range(4):
            for z in range(8):
                for c in range(2):
                    pairs.append((place(x, y, z, c), place(*target(x, y, z, c))))
    return lax.ppermute(value, AXES, pairs)


def way(c):
    return 1 - 2 * c


def x_out(x, y, z, c):
    return x + way(c), y, z, c


def x_back(x, y, z, c):
    return x - way(c), y, z, c


def y_out(x, y, z, c):
    return x, y + way(c), z, c


def y_back(x, y, z, c):
    return x, y - way(c), z, c


def z_out(x, y, z, c):
    return x, y, z + 2 * way(c), c


def z_back(x, y, z, c):
    return x, y, z - 2 * way(c), c


def z_swap(x, y, z, c):
    return x, y, z ^ 1, c


def core_swap(x, y, z, c):
    return x, y, z, 1 - c


MOVES = {x_out: (1, 0, 0), x_back: (-1, 0, 0), y_out: (1, 0, 0), y_back: (-1, 0, 0), z_out: (0, 1, 0), z_back: (0, -1, 0), z_swap: (0, 1, 0), core_swap: (0, 0, 1)}


def silu_product(gate, up):
    return (jax.nn.silu(gate.astype(jnp.float32)) * up.astype(jnp.float32)).astype(jnp.bfloat16)


def rows_kernel(gate, up, out):
    gated = gate[...].astype(jnp.float32)
    formed = gated / (1.0 + jnp.exp(-gated)) * up[...].astype(jnp.float32)
    out[0] = formed.T.astype(jnp.bfloat16)


def form_rows(gate, up):
    tokens, units = gate.shape
    return pl.pallas_call(
        rows_kernel,
        out_shape=jax.ShapeDtypeStruct((1, units, tokens), jnp.bfloat16),
        in_specs=[VMEM, VMEM],
        out_specs=VMEM,
        cost_estimate=pl.CostEstimate(flops=8 * gate.size, bytes_accessed=6 * gate.size, transcendentals=gate.size),
    )(gate, up)


def add_up(n, ready, left, cols, acc, first, first_ready, first_scale, scale, out, out_sems):
    units = acc.shape[0]
    done = []
    for index in range(n):
        ready(index)
        for step in range(units // CHUNK):
            part = pl.ds(step * CHUNK, CHUNK)
            product = jnp.dot(left(index, part), cols[index], preferred_element_type=jnp.float32)
            if index == 0:
                acc[part, :] = product
            elif index < n - 1:
                acc[part, :] += product
            else:
                if step == 0:
                    first_ready()
                acc[part, :] = first_scale * first[part, :] + scale * (acc[part, :] + product)
                done.append(pltpu.make_async_copy(acc.at[part], out.at[part], out_sems.at[step]))
                done[-1].start()
    for copy in done:
        copy.wait()


def early_kernel(n_pieces, n_columns, scale, table, hessian, *refs):
    pieces, columns = refs[:n_pieces], refs[n_pieces:n_pieces + n_columns]
    out, late_rows, rows, cols, old, acc, row_sems, col_sems, old_sem, late_sems, out_sems = refs[n_pieces + n_columns:]
    n_blocks = rows.shape[0]
    shard_at = lambda i: table[n_blocks + i]
    col_copies = [pltpu.make_async_copy(block, cols.at[i], col_sems.at[i]) for i, block in enumerate(columns)]
    old_copy = pltpu.make_async_copy(hessian, old, old_sem)
    col_copies[0].start()
    k = 0
    for piece in pieces:
        for i in range(piece.shape[0]):
            at = table[k]
            pltpu.make_async_copy(piece.at[i], rows.at[at], row_sems.at[at]).start()
            k += 1
    for copy in col_copies[1:]:
        copy.start()
    old_copy.start()
    kept = []

    def rows_ready(index):
        for i in range(4):
            at = shard_at(index) * 4 + i
            pltpu.make_async_copy(rows.at[at], rows.at[at], row_sems.at[at]).wait()

    def ready(index):
        rows_ready(index)
        col_copies[index].wait()

    def old_ready():
        old_copy.wait()
        for j in range(late_rows.shape[0] // 4):
            rows_ready(n_columns + j)
            for i in range(4):
                at = shard_at(n_columns + j) * 4 + i
                kept.append(pltpu.make_async_copy(rows.at[at], late_rows.at[j * 4 + i], late_sems.at[j * 4 + i]))
                kept[-1].start()

    def left(index, part):
        at = shard_at(index) * 4
        return jnp.concatenate([rows[at + i, part, :] for i in range(4)], axis=1)

    add_up(n_columns, ready, left, cols, acc, old, old_ready, 0.5, scale, out, out_sems)
    for copy in kept:
        copy.wait()


def late_kernel(n_columns, scale, partial, late_rows, *refs):
    columns = refs[:n_columns]
    out, rows, cols, old, acc, row_sems, col_sems, old_sem, out_sems = refs[n_columns:]
    row_copies, col_copies = [], []
    for i, block in enumerate(columns):
        own = pl.ds(i * 4, 4)
        row_copies.append(pltpu.make_async_copy(late_rows.at[own], rows.at[own], row_sems.at[i]))
        col_copies.append(pltpu.make_async_copy(block, cols.at[i], col_sems.at[i]))
        row_copies[-1].start()
        col_copies[-1].start()
    old_copy = pltpu.make_async_copy(partial, old, old_sem)
    old_copy.start()

    def ready(index):
        row_copies[index].wait()
        col_copies[index].wait()

    def left(index, part):
        return jnp.concatenate([rows[index * 4 + i, part, :] for i in range(4)], axis=1)

    add_up(n_columns, ready, left, cols, acc, old, old_copy.wait, 1.0, scale, out, out_sems)


def cost(columns, units):
    k = sum(b.shape[0] for b in columns)
    wide = columns[0].shape[1]
    return pl.CostEstimate(flops=2 * k * units * wide, bytes_accessed=8 * units * wide + 2 * k * (units + wide), transcendentals=0)


def body(hessian_old, gate_rows, up_rows, gate_columns, up_columns):
    tokens = lax.axis_size("col") * gate_rows.shape[0]
    row, col = lax.axis_index("row"), lax.axis_index("col")
    zl, x = row // 4, row % 4
    zh, y, c = col // 8, (col // 2) % 4, col % 2
    w = way(c)
    cat = lambda *blocks: jnp.concatenate(blocks, axis=0)

    r0 = form_rows(gate_rows, up_rows)
    own = silu_product(gate_columns, up_columns)

    plan = (
        ("za", ("r0",), z_out),
        ("ya1", ("r0",), y_out),
        ("yb1", ("r0",), y_back),
        ("zb", ("r0",), z_back),
        ("xb", ("own",), x_back),
        ("za",),
        ("zf", ("za",), z_out),
        ("ya1",),
        ("yf1", ("ya1",), y_out),
        ("yb1",),
        ("xa", ("own",), x_out),
        ("zb",),
        ("pair", ("own",), z_swap),
        ("xb",),
        ("ya2", ("za", "zb", "zf",), y_out),
        ("zf",),
        ("k1", ("ya1", "yb1", "yf1",), core_swap),
        ("yf1",),
        ("xf", ("xa",), x_out),
        ("xa",),
        ("yb2", ("za", "zb", "zf",), y_back),
        ("pair",),
        ("yf2", ("ya2",), y_out),
        ("ya2",),
        ("xb2", ("pair",), x_back),
        ("k1",),
        ("xf2", ("xf",), z_swap),
        ("xf",),
        ("k0", ("r0", "za", "zb", "zf",), core_swap),
        ("yb2",),
        ("xa2", ("pair",), x_out),
        ("yf2",),
        ("k2", ("ya2", "yb2", "yf2",), core_swap),
        ("k0",),
        ("k2",),
    )
    got = {"r0": r0, "own": own}
    came = {"r0": [(0, 0, 0)], "own": [(0, 0, 0)]}
    for name, *way_there in plan:
        if way_there:
            sources, target = way_there
            move = MOVES[target]
            came[name] = [tuple(p + q for p, q in zip(at, move)) for k in sources for at in came[k]]
    early_names, late_names = ("own", "pair", "xa", "xb", "xf",), ("xa2", "xb2", "xf2",)
    piece_names = ["r0"] + [name for name in came if name[0] in "zyk"]

    def token_block(side, up, other):
        sign = w * (1 - 2 * other)
        return ((zh - sign * up) % 4) * 8 + ((y - sign * side) % 4) * 2 + (c + other) % 2

    def shard(side, up, other):
        return ((zl + up) % 2) * 4 + (x - w * side) % 4

    block_at = [token_block(*at) for name in piece_names for at in came[name]]
    shard_at = [shard(*came[name][0]) for name in early_names + late_names]
    table = jnp.stack(block_at + shard_at).astype(jnp.int32) - 16
    for name, *way_there in plan:
        if way_there:
            sources, target = way_there
            value = got[sources[0]] if len(sources) == 1 else cat(*(got[k] for k in sources))
            table, value = lax.optimization_barrier((table, value))
            got[name] = send(value, target)
        else:
            table, got[name] = lax.optimization_barrier((table + 1, got[name]))

    pieces = [got[name] for name in piece_names]
    early = [got[name] for name in early_names]
    late = [got[name] for name in late_names]
    units, wide = hessian_old.shape
    scale = 1.0 / tokens
    n_blocks = tokens // 128
    n_late = 4 * len(late)
    params = pltpu.CompilerParams(vmem_limit_bytes=58 * 2**20)
    whole = pltpu.VMEM(hessian_old.shape, jnp.float32)
    dma = pltpu.SemaphoreType.DMA
    partial, late_rows = pl.pallas_call(
        functools.partial(early_kernel, len(pieces), len(early), scale),
        out_shape=(jax.ShapeDtypeStruct(hessian_old.shape, jnp.float32), jax.ShapeDtypeStruct((n_late, units, 128), jnp.bfloat16)),
        in_specs=[SMEM, HBM] + [HBM] * (len(pieces) + len(early)),
        out_specs=(HBM, HBM),
        scratch_shapes=[
            pltpu.VMEM((n_blocks, units, 128), jnp.bfloat16),
            pltpu.VMEM((len(early), *own.shape), jnp.bfloat16),
            whole,
            whole,
            dma((n_blocks,)),
            dma((len(early),)),
            dma,
            dma((n_late,)),
            dma((units // CHUNK,)),
        ],
        compiler_params=params,
        cost_estimate=cost(early, units),
    )(table, hessian_old, *pieces, *early)
    partial, *late = lax.optimization_barrier((partial, *late))
    return pl.pallas_call(
        functools.partial(late_kernel, len(late), scale),
        out_shape=jax.ShapeDtypeStruct(hessian_old.shape, jnp.float32),
        in_specs=[HBM] * (2 + len(late)),
        out_specs=HBM,
        scratch_shapes=[
            pltpu.VMEM((n_late, units, 128), jnp.bfloat16),
            pltpu.VMEM((len(late), *own.shape), jnp.bfloat16),
            whole,
            whole,
            dma((len(late),)),
            dma((len(late),)),
            dma,
            dma((units // CHUNK,)),
        ],
        compiler_params=params,
        cost_estimate=cost(late, units),
    )(partial, late_rows, *late)


def solution(mesh):
    in_specs = (P("row", "col"), P("col", "row"), P("col", "row"), P("row", "col"), P("row", "col"))
    out_specs = P("row", "col")
    return jax.shard_map(body, mesh=mesh, in_specs=in_specs, out_specs=out_specs, check_vma=False)
```

time: 187 us -> 97.8 us (0.52)
  waiting for transfers between devices: 156 us -> 35.6 us
  starting transfers between devices: 0.04 us -> 36.8 us
  Pallas kernels: 0 us -> 19.6 us
  between operations: 13.4 us -> 0.46 us
  matrix products: 12.6 us -> 0 us
  local copies, waits for them, and re-layouts: 0.01 us -> 2.03 us
    all_gather x2 -> x0, waiting for transfers between devices: 156 us -> none  [the longest x1 77.9 us: body(): lax.all_gather(row_formed, 'col', axis=0, tiled=True)]
    ppermute x0 -> x19, starting transfers between devices: none -> 36.8 us  [send(): return lax.ppermute(value, AXES, pairs)]
    ppermute x0 -> x19, waiting for transfers between devices: none -> 35.6 us  [send(): return lax.ppermute(value, AXES, pairs)]
    pallas_call x0 -> x3, Pallas kernels: none -> 19.6 us  [the longest x1 11.5 us: body(): pl.pallas_call(functools.partial(early_kernel, len(pieces), len(early), s...]
    dot_general x1 -> x0, matrix products: 12.6 us -> none  [body(): lax.dot_general(lax.all_gather(row_formed, 'col', axis=0, tiled=True), co...]
    unnamed x4 -> x38, local copies, waits for them, and re-layouts: 0.01 us -> 1.91 us
  transfers between devices with their start and end apart: 2 -> 19, of which waited for: 2 -> 9; matrix products, arithmetic and copies ran while one was open for 0% -> 3% of each run, Pallas kernels for 0% -> 12%
where the time goes in v2:
time: 97.8 us; the launch traced here: 97.6 us
  starting transfers between devices  36.8 us (38%)
  waiting for transfers between devices  35.6 us (36%)
  Pallas kernels  19.6 us (20%)
  other arithmetic  3.08 us (3%)
  local copies, waits for them, and re-layouts  2.03 us (2%)
    ppermute x19, starting transfers between devices, send(): return lax.ppermute(value, AXES, pairs)  36.8 us
    ppermute x19, waiting for transfers between devices, send(): return lax.ppermute(value, AXES, pairs)  35.6 us
    pallas_call x1, Pallas kernels, body(): pl.pallas_call(functools.partial(early_kernel, len(pieces), len(early), s...  11.5 us
    pallas_call x1, Pallas kernels, body(): pl.pallas_call(functools.partial(late_kernel, len(late), scale), out_shap...  6.15 us
    pallas_call x1, Pallas kernels, form_rows(): pl.pallas_call(rows_kernel, out_shape=jax.ShapeDtypeStruct((1, units, tok...  1.98 us
  transfers between devices with their start and end apart: 19, of which 9 were waited for; matrix products, arithmetic and copies ran while one was open for 3% of the time, Pallas kernels for 12%

profile of v2, /device:TPU:1, one launch (start us, length us, event | category | flops | bytes accessed | tf_op | source)
XLA Modules:
  0.0 97.6 jit_solution(11094798721313569589)
XLA Ops:
  0.0 0.1 stack.163
  0.1 2.0 %shard_map.55.refs_0_ = bf16[1,1024,128]{2,1,0:T(8,128)(2,1)} custom-call(bf16[128,1024]{1,0:T(8,128)(2,1)} %gate.1, bf16[128,1024]{1,0:T(8,128)(2,1)} %up.1), custom_call_target="tpu_custom_call" | custom-call | flops 1048576 | bytes 786432 | tf_op jit(solution)/shard_map/pallas_call | solution.py:85
  2.1 6.8 %collective-permute-start = (bf16[1,1024,128]{2,1,0:T(8,128)(2,1)}, bf16[1,1024,128]{2,1,0:T(8,128)(2,1)S(1)}, u32[]{:S(2)}, u32[]{:S(2)}) collective-permute-start(bf16[1,1024,128]{2,1,0:T(8,128)(2,1)} %shard_map.55.refs_0_), channel_id=1, source_target_pairs={{0,8},{1,25},{128,136},{129,153},{8,16},{9,1},{136,144},{137,129},... | collective-permute-start | bytes 786440 | tf_op jit(solution)/shard_map/ppermute | solution.py:31
  9.0 2.7 %collective-permute-start.1 = (bf16[1,1024,128]{2,1,0:T(8,128)(2,1)}, bf16[1,1024,128]{2,1,0:T(8,128)(2,1)S(1)}, u32[]{:S(2)}, u32[]{:S(2)}) collective-permute-start(bf16[1,1024,128]{2,1,0:T(8,128)(2,1)} %shard_map.55.refs_0_), channel_id=1, source_target_pairs={{0,2},{1,7},{128,130},{129,135},{8,10},{9,15},{136,138},{137,143},... | collective-permute-start | bytes 786440 | tf_op jit(solution)/shard_map/ppermute | solution.py:31
  11.7 0.0 collective-permute-start.2
  11.7 0.0 collective-permute-start.3
  11.7 1.9 %fusion.4.refs_13_ = bf16[512,768]{1,0:T(8,128)(2,1)S(1)} fusion(bf16[512,768]{1,0:T(8,128)(2,1)} %param.9, bf16[512,768]{1,0:T(8,128)(2,1)} %param.8), kind=kLoop, calls=%fused_computation.7 | loop fusion | flops 3145728 | bytes 2359296 | tf_op jit(solution)/shard_map/convert_element_type | solution.py:74
  13.6 0.0 copy-start.6
  13.6 1.3 %collective-permute-start.4 = (bf16[512,768]{1,0:T(8,128)(2,1)S(1)}, bf16[512,768]{1,0:T(8,128)(2,1)S(1)}, u32[]{:S(2)}, u32[]{:S(2)}) collective-permute-start(bf16[512,768]{1,0:T(8,128)(2,1)S(1)} %fusion.4.refs_13_), channel_id=1, source_target_pairs={{0,96},{1,33},{128,224},{129,161},{8,104},{9,41},{136,232},{137,16... | collective-permute-start | bytes 2359304 | tf_op jit(solution)/shard_map/ppermute | solution.py:31
  14.9 4.1 %collective-permute-done.refs_1_ = bf16[1,1024,128]{2,1,0:T(8,128)(2,1)S(1)} collective-permute-done((bf16[1,1024,128]{2,1,0:T(8,128)(2,1)}, bf16[1,1024,128]{2,1,0:T(8,128)(2,1)S(1)}, u32[]{:S(2)}, u32[]{:S(2)}) %collective-permute-start) | collective-permute-done | bytes 262176 | tf_op jit(solution)/shard_map/ppermute | solution.py:31
  19.0 0.0 collective-permute-done.1.refs_2_
  19.0 0.0 collective-permute-done.2.refs_3_
  19.0 4.4 %collective-permute-start.5 = (bf16[1,1024,128]{2,1,0:T(8,128)(2,1)S(1)}, bf16[1,1024,128]{2,1,0:T(8,128)(2,1)S(1)}, u32[]{:S(2)}, u32[]{:S(2)}) collective-permute-start(bf16[1,1024,128]{2,1,0:T(8,128)(2,1)S(1)} %collective-permute-done.refs_1_), channel_id=1, source_target_pairs={{0,8},{1,25},{128,136},{129,153},{8,16},{9,1},{136,144},{137,129},... | collective-permute-start | bytes 786440 | tf_op jit(solution)/shard_map/ppermute | solution.py:31
  23.5 0.0 collective-permute-done.3.refs_4_
  23.5 2.6 %collective-permute-start.6 = (bf16[1,1024,128]{2,1,0:T(8,128)(2,1)S(1)}, bf16[1,1024,128]{2,1,0:T(8,128)(2,1)S(1)}, u32[]{:S(2)}, u32[]{:S(2)}) collective-permute-start(bf16[1,1024,128]{2,1,0:T(8,128)(2,1)S(1)} %collective-permute-done.1.refs_2_), channel_id=1, source_target_pairs={{0,2},{1,7},{128,130},{129,135},{8,10},{9,15},{136,138},{137,143},... | collective-permute-start | bytes 786440 | tf_op jit(solution)/shard_map/ppermute | solution.py:31
  26.1 2.5 %collective-permute-start.7 = (bf16[512,768]{1,0:T(8,128)(2,1)S(1)}, bf16[512,768]{1,0:T(8,128)(2,1)S(1)}, u32[]{:S(2)}, u32[]{:S(2)}) collective-permute-start(bf16[512,768]{1,0:T(8,128)(2,1)S(1)} %fusion.4.refs_13_), channel_id=1, source_target_pairs={{0,32},{1,97},{128,160},{129,225},{8,40},{9,105},{136,168},{137,23... | collective-permute-start | bytes 2359304 | tf_op jit(solution)/shard_map/ppermute | solution.py:31
  28.5 0.0 collective-permute-start.8
  28.5 0.0 collective-permute-done.5.refs_5_
  28.5 0.0 copy-start.2
  28.6 0.1 pad_maximum_fusion.2
  28.7 0.7 collective-permute-done.6.refs_6_
  29.4 0.1 pad_maximum_fusion.4
  29.5 0.0 collective-permute-done.4.refs_16_
  29.5 3.5 %collective-permute-start.9 = (bf16[3,1024,128]{2,1,0:T(8,128)(2,1)S(1)}, bf16[3,1024,128]{2,1,0:T(8,128)(2,1)S(1)}, u32[]{:S(2)}, u32[]{:S(2)}) collective-permute-start(bf16[3,1024,128]{2,1,0:T(8,128)(2,1)S(1)} %pad_maximum_fusion.2), channel_id=1, source_target_pairs={{0,2},{1,7},{128,130},{129,135},{8,10},{9,15},{136,138},{137,143},... | collective-permute-start | bytes 2359304 | tf_op jit(solution)/shard_map/ppermute | solution.py:31
  33.0 0.9 collective-permute-start.10
  33.9 0.1 pad_maximum_fusion.5
  33.9 0.0 copy-done.6
  34.0 0.0 copy-done
  34.0 0.0 copy-done.9
  34.0 0.0 copy-done.10
  34.0 0.0 copy-done.1
  34.0 0.0 copy-done.2
  34.0 0.0 copy-done.7
  34.0 0.1 pad_maximum_fusion.1
  34.2 3.3 %collective-permute-done.7.refs_15_ = bf16[512,768]{1,0:T(8,128)(2,1)S(1)} collective-permute-done((bf16[512,768]{1,0:T(8,128)(2,1)S(1)}, bf16[512,768]{1,0:T(8,128)(2,1)S(1)}, u32[]{:S(2)}, u32[]{:S(2)}) %collective-permute-start.7) | collective-permute-done | bytes 786464 | tf_op jit(solution)/shard_map/ppermute | solution.py:31
  37.5 3.4 %collective-permute-start.11 = (bf16[512,768]{1,0:T(8,128)(2,1)S(1)}, bf16[512,768]{1,0:T(8,128)(2,1)}, u32[]{:S(2)}, u32[]{:S(2)}) collective-permute-start(bf16[512,768]{1,0:T(8,128)(2,1)S(1)} %collective-permute-done.7.refs_15_), channel_id=1, source_target_pairs={{0,32},{1,97},{128,160},{129,225},{8,40},{9,105},{136,168},{137,23... | collective-permute-start | bytes 2359304 | tf_op jit(solution)/shard_map/ppermute | solution.py:31
  40.9 6.2 %collective-permute-done.8.refs_14_ = bf16[512,768]{1,0:T(8,128)(2,1)S(1)} collective-permute-done((bf16[512,768]{1,0:T(8,128)(2,1)S(1)}, bf16[512,768]{1,0:T(8,128)(2,1)S(1)}, u32[]{:S(2)}, u32[]{:S(2)}) %collective-permute-start.8) | collective-permute-done | bytes 786464 | tf_op jit(solution)/shard_map/ppermute | solution.py:31
  47.1 0.0 collective-permute-start.12
  47.1 0.0 collective-permute-done.9.refs_7_
  47.1 0.0 copy-start.3
  47.1 2.9 %collective-permute-start.13 = (bf16[3,1024,128]{2,1,0:T(8,128)(2,1)S(1)}, bf16[3,1024,128]{2,1,0:T(8,128)(2,1)S(1)}, u32[]{:S(2)}, u32[]{:S(2)}) collective-permute-start(bf16[3,1024,128]{2,1,0:T(8,128)(2,1)S(1)} %collective-permute-done.9.refs_7_), channel_id=1, source_target_pairs={{0,2},{1,7},{128,130},{129,135},{8,10},{9,15},{136,138},{137,143},... | collective-permute-start | bytes 2359304 | tf_op jit(solution)/shard_map/ppermute | solution.py:31
  50.0 0.0 collective-permute-done.10.refs_8_
  50.1 0.0 collective-permute-done.11.refs_17_
  50.1 15.4 %collective-permute-done.12.refs_9_ = bf16[3,1024,128]{2,1,0:T(8,128)(2,1)S(1)} collective-permute-done((bf16[3,1024,128]{2,1,0:T(8,128)(2,1)S(1)}, bf16[3,1024,128]{2,1,0:T(8,128)(2,1)S(1)}, u32[]{:S(2)}, u32[]{:S(2)}) %collective-permute-start.12) | collective-permute-done | bytes 786464 | tf_op jit(solution)/shard_map/ppermute | solution.py:31
  65.5 1.4 %collective-permute-done.13.refs_10_ = bf16[3,1024,128]{2,1,0:T(8,128)(2,1)S(1)} collective-permute-done((bf16[3,1024,128]{2,1,0:T(8,128)(2,1)S(1)}, bf16[3,1024,128]{2,1,0:T(8,128)(2,1)S(1)}, u32[]{:S(2)}, u32[]{:S(2)}) %collective-permute-start.13) | collective-permute-done | bytes 786464 | tf_op jit(solution)/shard_map/ppermute | solution.py:31
  66.9 0.3 pad_maximum_fusion
  67.2 0.0 copy-done.13
  67.2 0.0 copy-done.15
  67.2 0.0 copy-done.3
  67.2 1.4 %collective-permute-start.15 = (bf16[9,1024,128]{2,1,0:T(8,128)(2,1)S(1)}, bf16[9,1024,128]{2,1,0:T(8,128)(2,1)S(1)}, u32[]{:S(2)}, u32[]{:S(2)}) collective-permute-start(bf16[9,1024,128]{2,1,0:T(8,128)(2,1)S(1)} %pad_maximum_fusion), channel_id=1, source_target_pairs={{0,1},{1,0},{128,129},{129,128},{8,9},{9,8},{136,137},{137,136},{1... | collective-permute-start | bytes 7077896 | tf_op jit(solution)/shard_map/ppermute | solution.py:31
  68.7 0.1 collective-permute-start.14
  68.8 0.0 collective-permute-start.17
  68.8 2.7 %collective-permute-start.16 = (bf16[512,768]{1,0:T(8,128)(2,1)S(1)}, bf16[512,768]{1,0:T(8,128)(2,1)S(1)}, u32[]{:S(2)}, u32[]{:S(2)}) collective-permute-start(bf16[512,768]{1,0:T(8,128)(2,1)S(1)} %collective-permute-done.8.refs_14_), channel_id=1, source_target_pairs={{0,32},{1,97},{128,160},{129,225},{8,40},{9,105},{136,168},{137,23... | collective-permute-start | bytes 2359304 | tf_op jit(solution)/shard_map/ppermute | solution.py:31
  71.4 1.6 %collective-permute-start.18 = (bf16[512,768]{1,0:T(8,128)(2,1)}, bf16[512,768]{1,0:T(8,128)(2,1)}, u32[]{:S(2)}, u32[]{:S(2)}) collective-permute-start(bf16[512,768]{1,0:T(8,128)(2,1)} %collective-permute-done.11.refs_17_), channel_id=1, source_target_pairs={{0,128},{1,129},{128,0},{129,1},{8,136},{9,137},{136,8},{137,9},{1... | collective-permute-start | bytes 2359304 | tf_op jit(solution)/shard_map/ppermute | solution.py:31
  73.0 1.3 %collective-permute-done.14.refs_11_ = bf16[4,1024,128]{2,1,0:T(8,128)(2,1)S(1)} collective-permute-done((bf16[4,1024,128]{2,1,0:T(8,128)(2,1)S(1)}, bf16[4,1024,128]{2,1,0:T(8,128)(2,1)S(1)}, u32[]{:S(2)}, u32[]{:S(2)}) %collective-permute-start.14) | collective-permute-done | bytes 1048608 | tf_op jit(solution)/shard_map/ppermute | solution.py:31
  74.3 0.5 broadcast_add_fusion.table
  74.9 0.0 collective-permute-done.15.refs_12_
  74.9 0.4 copy-done.12
  75.3 1.4 %copy-done.8 = bf16[9,1024,128]{2,1,0:T(8,128)(2,1)} copy-done((bf16[9,1024,128]{2,1,0:T(8,128)(2,1)}, bf16[9,1024,128]{2,1,0:T(8,128)(2,1)S(1)}, u32[]{:S(2)}) %copy-start.8) | copy-done | bytes 2359320
  76.7 11.5 %shard_map.56 = (f32[1024,768]{1,0:T(8,128)}, bf16[12,1024,128]{2,1,0:T(8,128)(2,1)}) custom-call(s32[40]{0:T(128)} %broadcast_add_fusion.table, f32[1024,768]{1,0:T(8,128)} %hessian.1, bf16[1,1024,128]{2,1,0:T(8,128)(2,1)} %shard_map.55.refs_0_, bf16[1,1024,128]{2,1,0:T(8,128)(2,1)} %copy-done, bf16[1,1024,128]{2,1,0:T(8,128)(2,1)} %copy-done.9, ...), custom_call_target="tpu_custom_call" | custom-call | flops 4026531840 | bytes 15466496 | tf_op jit(solution)/shard_map/pallas_call | solution.py:278
  88.2 0.0 collective-permute-done.17.refs_1_
  88.2 0.2 collective-permute-done.16.refs_0_
  88.5 2.9 %collective-permute-done.18.refs_2_ = bf16[512,768]{1,0:T(8,128)(2,1)} collective-permute-done((bf16[512,768]{1,0:T(8,128)(2,1)}, bf16[512,768]{1,0:T(8,128)(2,1)}, u32[]{:S(2)}, u32[]{:S(2)}) %collective-permute-start.18) | collective-permute-done | bytes 786464 | tf_op jit(solution)/shard_map/ppermute | solution.py:31
  91.3 6.2 %shard_map.57 = f32[1024,768]{1,0:T(8,128)} custom-call(f32[1024,768]{1,0:T(8,128)} %get-tuple-element.148.partial, bf16[12,1024,128]{2,1,0:T(8,128)(2,1)} %get-tuple-element.149.late_rows, bf16[512,768]{1,0:T(8,128)(2,1)} %copy-done.18, bf16[512,768]{1,0:T(8,128)(2,1)} %copy-done.17, bf16[512,768]{1,0:T(8,128)(2,1)} %collective-permute-done.18.refs_2_), custom_call_target="tpu_custom_call" | custom-call | flops 2415919104 | bytes 11796480 | tf_op jit(solution)/shard_map/pallas_call | solution.py:298
  (39 shorter events, 0.1 us)
Async XLA Ops:
  2.1 16.9 %collective-permute-start = (bf16[1,1024,128]{2,1,0:T(8,128)(2,1)}, bf16[1,1024,128]{2,1,0:T(8,128)(2,1)S(1)}, u32[]{:S(2)}, u32[]{:S(2)}) collective-permute-start(bf16[1,1024,128]{2,1,0:T(8,128)(2,1)} %shard_map.55.refs_0_), channel_id=1, source_target_pairs={{0,8},{1,25},{128,136},{129,153},{8,16},{9,1},{136,144},{137,129},... | collective-permute-start | bytes 786440 | tf_op jit(solution)/shard_map/ppermute | solution.py:31
  9.0 10.0 %collective-permute-start.1 = (bf16[1,1024,128]{2,1,0:T(8,128)(2,1)}, bf16[1,1024,128]{2,1,0:T(8,128)(2,1)S(1)}, u32[]{:S(2)}, u32[]{:S(2)}) collective-permute-start(bf16[1,1024,128]{2,1,0:T(8,128)(2,1)} %shard_map.55.refs_0_), channel_id=1, source_target_pairs={{0,2},{1,7},{128,130},{129,135},{8,10},{9,15},{136,138},{137,143},... | collective-permute-start | bytes 786440 | tf_op jit(solution)/shard_map/ppermute | solution.py:31
  11.7 7.3 %collective-permute-start.2 = (bf16[1,1024,128]{2,1,0:T(8,128)(2,1)}, bf16[1,1024,128]{2,1,0:T(8,128)(2,1)S(1)}, u32[]{:S(2)}, u32[]{:S(2)}) collective-permute-start(bf16[1,1024,128]{2,1,0:T(8,128)(2,1)} %shard_map.55.refs_0_), channel_id=1, source_target_pairs={{0,6},{1,3},{128,134},{129,131},{8,14},{9,11},{136,142},{137,139},... | collective-permute-start | bytes 786440 | tf_op jit(solution)/shard_map/ppermute | solution.py:31
  11.7 11.8 %collective-permute-start.3 = (bf16[1,1024,128]{2,1,0:T(8,128)(2,1)}, bf16[1,1024,128]{2,1,0:T(8,128)(2,1)S(1)}, u32[]{:S(2)}, u32[]{:S(2)}) collective-permute-start(bf16[1,1024,128]{2,1,0:T(8,128)(2,1)} %shard_map.55.refs_0_), channel_id=1, source_target_pairs={{0,24},{1,9},{128,152},{129,137},{8,0},{9,17},{136,128},{137,145},... | collective-permute-start | bytes 786440 | tf_op jit(solution)/shard_map/ppermute | solution.py:31
  13.6 20.4 %copy-start.6 = (bf16[512,768]{1,0:T(8,128)(2,1)}, bf16[512,768]{1,0:T(8,128)(2,1)S(1)}, u32[]{:S(2)}) copy-start(bf16[512,768]{1,0:T(8,128)(2,1)S(1)} %fusion.4.refs_13_) | copy-start | bytes 2359300
  13.6 15.9 %collective-permute-start.4 = (bf16[512,768]{1,0:T(8,128)(2,1)S(1)}, bf16[512,768]{1,0:T(8,128)(2,1)S(1)}, u32[]{:S(2)}, u32[]{:S(2)}) collective-permute-start(bf16[512,768]{1,0:T(8,128)(2,1)S(1)} %fusion.4.refs_13_), channel_id=1, source_target_pairs={{0,96},{1,33},{128,224},{129,161},{8,104},{9,41},{136,232},{137,16... | collective-permute-start | bytes 2359304 | tf_op jit(solution)/shard_map/ppermute | solution.py:31
  19.0 15.0 %copy-start = (bf16[1,1024,128]{2,1,0:T(8,128)(2,1)}, bf16[1,1024,128]{2,1,0:T(8,128)(2,1)S(1)}, u32[]{:S(2)}) copy-start(bf16[1,1024,128]{2,1,0:T(8,128)(2,1)S(1)} %collective-permute-done.refs_1_) | copy-start | bytes 786436
  19.0 15.0 %copy-start.9 = (bf16[1,1024,128]{2,1,0:T(8,128)(2,1)}, bf16[1,1024,128]{2,1,0:T(8,128)(2,1)S(1)}, u32[]{:S(2)}) copy-start(bf16[1,1024,128]{2,1,0:T(8,128)(2,1)S(1)} %collective-permute-done.1.refs_2_) | copy-start | bytes 786436
  19.0 14.9 %copy-start.10 = (bf16[1,1024,128]{2,1,0:T(8,128)(2,1)}, bf16[1,1024,128]{2,1,0:T(8,128)(2,1)S(1)}, u32[]{:S(2)}) copy-start(bf16[1,1024,128]{2,1,0:T(8,128)(2,1)S(1)} %collective-permute-done.2.refs_3_) | copy-start | bytes 786436
  19.0 9.5 %collective-permute-start.5 = (bf16[1,1024,128]{2,1,0:T(8,128)(2,1)S(1)}, bf16[1,1024,128]{2,1,0:T(8,128)(2,1)S(1)}, u32[]{:S(2)}, u32[]{:S(2)}) collective-permute-start(bf16[1,1024,128]{2,1,0:T(8,128)(2,1)S(1)} %collective-permute-done.refs_1_), channel_id=1, source_target_pairs={{0,8},{1,25},{128,136},{129,153},{8,16},{9,1},{136,144},{137,129},... | collective-permute-start | bytes 786440 | tf_op jit(solution)/shard_map/ppermute | solution.py:31
  23.5 10.5 %copy-start.1 = (bf16[1,1024,128]{2,1,0:T(8,128)(2,1)}, bf16[1,1024,128]{2,1,0:T(8,128)(2,1)S(1)}, u32[]{:S(2)}) copy-start(bf16[1,1024,128]{2,1,0:T(8,128)(2,1)S(1)} %collective-permute-done.3.refs_4_) | copy-start | bytes 786436
  23.5 5.9 %collective-permute-start.6 = (bf16[1,1024,128]{2,1,0:T(8,128)(2,1)S(1)}, bf16[1,1024,128]{2,1,0:T(8,128)(2,1)S(1)}, u32[]{:S(2)}, u32[]{:S(2)}) collective-permute-start(bf16[1,1024,128]{2,1,0:T(8,128)(2,1)S(1)} %collective-permute-done.1.refs_2_), channel_id=1, source_target_pairs={{0,2},{1,7},{128,130},{129,135},{8,10},{9,15},{136,138},{137,143},... | collective-permute-start | bytes 786440 | tf_op jit(solution)/shard_map/ppermute | solution.py:31
  26.1 11.4 %collective-permute-start.7 = (bf16[512,768]{1,0:T(8,128)(2,1)S(1)}, bf16[512,768]{1,0:T(8,128)(2,1)S(1)}, u32[]{:S(2)}, u32[]{:S(2)}) collective-permute-start(bf16[512,768]{1,0:T(8,128)(2,1)S(1)} %fusion.4.refs_13_), channel_id=1, source_target_pairs={{0,32},{1,97},{128,160},{129,225},{8,40},{9,105},{136,168},{137,23... | collective-permute-start | bytes 2359304 | tf_op jit(solution)/shard_map/ppermute | solution.py:31
  28.5 18.6 %collective-permute-start.8 = (bf16[512,768]{1,0:T(8,128)(2,1)S(1)}, bf16[512,768]{1,0:T(8,128)(2,1)S(1)}, u32[]{:S(2)}, u32[]{:S(2)}) collective-permute-start(bf16[512,768]{1,0:T(8,128)(2,1)S(1)} %fusion.4.refs_13_), channel_id=1, source_target_pairs={{0,128},{1,129},{128,0},{129,1},{8,136},{9,137},{136,8},{137,9},{1... | collective-permute-start | bytes 2359304 | tf_op jit(solution)/shard_map/ppermute | solution.py:31
  28.5 5.5 %copy-start.7 = (bf16[1,1024,128]{2,1,0:T(8,128)(2,1)S(1)}, bf16[1,1024,128]{2,1,0:T(8,128)(2,1)}, u32[]{:S(2)}) copy-start(bf16[1,1024,128]{2,1,0:T(8,128)(2,1)} %shard_map.55.refs_0_) | copy-start | bytes 786436
  28.5 5.5 %copy-start.2 = (bf16[1,1024,128]{2,1,0:T(8,128)(2,1)}, bf16[1,1024,128]{2,1,0:T(8,128)(2,1)S(1)}, u32[]{:S(2)}) copy-start(bf16[1,1024,128]{2,1,0:T(8,128)(2,1)S(1)} %collective-permute-done.5.refs_5_) | copy-start | bytes 786436
  29.4 4.8 %copy-start.11 = (bf16[1,1024,128]{2,1,0:T(8,128)(2,1)}, bf16[1,1024,128]{2,1,0:T(8,128)(2,1)S(1)}, u32[]{:S(2)}) copy-start(bf16[1,1024,128]{2,1,0:T(8,128)(2,1)S(1)} %collective-permute-done.6.refs_6_) | copy-start | bytes 786436
  29.5 37.7 %copy-start.13 = (bf16[512,768]{1,0:T(8,128)(2,1)}, bf16[512,768]{1,0:T(8,128)(2,1)S(1)}, u32[]{:S(2)}) copy-start(bf16[512,768]{1,0:T(8,128)(2,1)S(1)} %collective-permute-done.4.refs_16_) | copy-start | bytes 2359300
  29.5 17.6 %collective-permute-start.9 = (bf16[3,1024,128]{2,1,0:T(8,128)(2,1)S(1)}, bf16[3,1024,128]{2,1,0:T(8,128)(2,1)S(1)}, u32[]{:S(2)}, u32[]{:S(2)}) collective-permute-start(bf16[3,1024,128]{2,1,0:T(8,128)(2,1)S(1)} %pad_maximum_fusion.2), channel_id=1, source_target_pairs={{0,2},{1,7},{128,130},{129,135},{8,10},{9,15},{136,138},{137,143},... | collective-permute-start | bytes 2359304 | tf_op jit(solution)/shard_map/ppermute | solution.py:31
  33.0 17.1 %collective-permute-start.10 = (bf16[3,1024,128]{2,1,0:T(8,128)(2,1)S(1)}, bf16[3,1024,128]{2,1,0:T(8,128)(2,1)S(1)}, u32[]{:S(2)}, u32[]{:S(2)}) collective-permute-start(bf16[3,1024,128]{2,1,0:T(8,128)(2,1)S(1)} %pad_maximum_fusion.4), channel_id=1, source_target_pairs={{0,1},{1,0},{128,129},{129,128},{8,9},{9,8},{136,137},{137,136},{1... | collective-permute-start | bytes 2359304 | tf_op jit(solution)/shard_map/ppermute | solution.py:31
  37.5 29.7 %copy-start.15 = (bf16[512,768]{1,0:T(8,128)(2,1)}, bf16[512,768]{1,0:T(8,128)(2,1)S(1)}, u32[]{:S(2)}) copy-start(bf16[512,768]{1,0:T(8,128)(2,1)S(1)} %collective-permute-done.7.refs_15_) | copy-start | bytes 2359300
  37.5 12.6 %collective-permute-start.11 = (bf16[512,768]{1,0:T(8,128)(2,1)S(1)}, bf16[512,768]{1,0:T(8,128)(2,1)}, u32[]{:S(2)}, u32[]{:S(2)}) collective-permute-start(bf16[512,768]{1,0:T(8,128)(2,1)S(1)} %collective-permute-done.7.refs_15_), channel_id=1, source_target_pairs={{0,32},{1,97},{128,160},{129,225},{8,40},{9,105},{136,168},{137,23... | collective-permute-start | bytes 2359304 | tf_op jit(solution)/shard_map/ppermute | solution.py:31
  47.1 21.7 %copy-start.14 = (bf16[512,768]{1,0:T(8,128)(2,1)}, bf16[512,768]{1,0:T(8,128)(2,1)S(1)}, u32[]{:S(2)}) copy-start(bf16[512,768]{1,0:T(8,128)(2,1)S(1)} %collective-permute-done.8.refs_14_) | copy-start | bytes 2359300
  47.1 18.4 %collective-permute-start.12 = (bf16[3,1024,128]{2,1,0:T(8,128)(2,1)S(1)}, bf16[3,1024,128]{2,1,0:T(8,128)(2,1)S(1)}, u32[]{:S(2)}, u32[]{:S(2)}) collective-permute-start(bf16[3,1024,128]{2,1,0:T(8,128)(2,1)S(1)} %pad_maximum_fusion.5), channel_id=1, source_target_pairs={{0,6},{1,3},{128,134},{129,131},{8,14},{9,11},{136,142},{137,139},... | collective-permute-start | bytes 2359304 | tf_op jit(solution)/shard_map/ppermute | solution.py:31
  47.1 20.1 %copy-start.3 = (bf16[3,1024,128]{2,1,0:T(8,128)(2,1)}, bf16[3,1024,128]{2,1,0:T(8,128)(2,1)S(1)}, u32[]{:S(2)}) copy-start(bf16[3,1024,128]{2,1,0:T(8,128)(2,1)S(1)} %collective-permute-done.9.refs_7_) | copy-start | bytes 2359300
  47.1 19.8 %collective-permute-start.13 = (bf16[3,1024,128]{2,1,0:T(8,128)(2,1)S(1)}, bf16[3,1024,128]{2,1,0:T(8,128)(2,1)S(1)}, u32[]{:S(2)}, u32[]{:S(2)}) collective-permute-start(bf16[3,1024,128]{2,1,0:T(8,128)(2,1)S(1)} %collective-permute-done.9.refs_7_), channel_id=1, source_target_pairs={{0,2},{1,7},{128,130},{129,135},{8,10},{9,15},{136,138},{137,143},... | collective-permute-start | bytes 2359304 | tf_op jit(solution)/shard_map/ppermute | solution.py:31
  50.1 16.9 %copy-start.16 = (bf16[3,1024,128]{2,1,0:T(8,128)(2,1)}, bf16[3,1024,128]{2,1,0:T(8,128)(2,1)S(1)}, u32[]{:S(2)}) copy-start(bf16[3,1024,128]{2,1,0:T(8,128)(2,1)S(1)} %collective-permute-done.10.refs_8_) | copy-start | bytes 2359300
  65.5 1.7 %copy-start.4 = (bf16[3,1024,128]{2,1,0:T(8,128)(2,1)}, bf16[3,1024,128]{2,1,0:T(8,128)(2,1)S(1)}, u32[]{:S(2)}) copy-start(bf16[3,1024,128]{2,1,0:T(8,128)(2,1)S(1)} %collective-permute-done.12.refs_9_) | copy-start | bytes 2359300
  66.9 6.1 %copy-start.5 = (bf16[3,1024,128]{2,1,0:T(8,128)(2,1)}, bf16[3,1024,128]{2,1,0:T(8,128)(2,1)S(1)}, u32[]{:S(2)}) copy-start(bf16[3,1024,128]{2,1,0:T(8,128)(2,1)S(1)} %collective-permute-done.13.refs_10_) | copy-start | bytes 2359300
  67.2 7.6 %collective-permute-start.15 = (bf16[9,1024,128]{2,1,0:T(8,128)(2,1)S(1)}, bf16[9,1024,128]{2,1,0:T(8,128)(2,1)S(1)}, u32[]{:S(2)}, u32[]{:S(2)}) collective-permute-start(bf16[9,1024,128]{2,1,0:T(8,128)(2,1)S(1)} %pad_maximum_fusion), channel_id=1, source_target_pairs={{0,1},{1,0},{128,129},{129,128},{8,9},{9,8},{136,137},{137,136},{1... | collective-permute-start | bytes 7077896 | tf_op jit(solution)/shard_map/ppermute | solution.py:31
  68.7 5.7 %collective-permute-start.14 = (bf16[4,1024,128]{2,1,0:T(8,128)(2,1)S(1)}, bf16[4,1024,128]{2,1,0:T(8,128)(2,1)S(1)}, u32[]{:S(2)}, u32[]{:S(2)}) collective-permute-start(bf16[4,1024,128]{2,1,0:T(8,128)(2,1)S(1)} %pad_maximum_fusion.1), channel_id=1, source_target_pairs={{0,1},{1,0},{128,129},{129,128},{8,9},{9,8},{136,137},{137,136},{1... | collective-permute-start | bytes 3145736 | tf_op jit(solution)/shard_map/ppermute | solution.py:31
  68.8 19.4 %collective-permute-start.17 = (bf16[512,768]{1,0:T(8,128)(2,1)S(1)}, bf16[512,768]{1,0:T(8,128)(2,1)S(1)}, u32[]{:S(2)}, u32[]{:S(2)}) collective-permute-start(bf16[512,768]{1,0:T(8,128)(2,1)S(1)} %collective-permute-done.8.refs_14_), channel_id=1, source_target_pairs={{0,96},{1,33},{128,224},{129,161},{8,104},{9,41},{136,232},{137,16... | collective-permute-start | bytes 2359304 | tf_op jit(solution)/shard_map/ppermute | solution.py:31
  68.8 19.7 %collective-permute-start.16 = (bf16[512,768]{1,0:T(8,128)(2,1)S(1)}, bf16[512,768]{1,0:T(8,128)(2,1)S(1)}, u32[]{:S(2)}, u32[]{:S(2)}) collective-permute-start(bf16[512,768]{1,0:T(8,128)(2,1)S(1)} %collective-permute-done.8.refs_14_), channel_id=1, source_target_pairs={{0,32},{1,97},{128,160},{129,225},{8,40},{9,105},{136,168},{137,23... | collective-permute-start | bytes 2359304 | tf_op jit(solution)/shard_map/ppermute | solution.py:31
  71.4 19.9 %collective-permute-start.18 = (bf16[512,768]{1,0:T(8,128)(2,1)}, bf16[512,768]{1,0:T(8,128)(2,1)}, u32[]{:S(2)}, u32[]{:S(2)}) collective-permute-start(bf16[512,768]{1,0:T(8,128)(2,1)} %collective-permute-done.11.refs_17_), channel_id=1, source_target_pairs={{0,128},{1,129},{128,0},{129,1},{8,136},{9,137},{136,8},{137,9},{1... | collective-permute-start | bytes 2359304 | tf_op jit(solution)/shard_map/ppermute | solution.py:31
  74.3 1.0 copy-start.12
  75.3 1.4 %copy-start.8 = (bf16[9,1024,128]{2,1,0:T(8,128)(2,1)}, bf16[9,1024,128]{2,1,0:T(8,128)(2,1)S(1)}, u32[]{:S(2)}) copy-start(bf16[9,1024,128]{2,1,0:T(8,128)(2,1)S(1)} %collective-permute-done.15.refs_12_) | copy-start | bytes 7077892
  88.2 3.1 %copy-start.17 = (bf16[512,768]{1,0:T(8,128)(2,1)}, bf16[512,768]{1,0:T(8,128)(2,1)S(1)}, u32[]{:S(2)}) copy-start(bf16[512,768]{1,0:T(8,128)(2,1)S(1)} %collective-permute-done.17.refs_1_) | copy-start | bytes 2359300
  88.5 2.9 %copy-start.18 = (bf16[512,768]{1,0:T(8,128)(2,1)}, bf16[512,768]{1,0:T(8,128)(2,1)S(1)}, u32[]{:S(2)}) copy-start(bf16[512,768]{1,0:T(8,128)(2,1)S(1)} %collective-permute-done.16.refs_0_) | copy-start | bytes 2359300

commit v3 on v2

--- a/solution.py
+++ b/solution.py
@@ -216,20 +216,20 @@
         ("xb",),
         ("ya2", ("za", "zb", "zf",), y_out),
         ("zf",),
-        ("k1", ("ya1", "yb1", "yf1",), core_swap),
+        ("yb2", ("za", "zb", "zf",), y_back),
         ("yf1",),
         ("xf", ("xa",), x_out),
         ("xa",),
-        ("yb2", ("za", "zb", "zf",), y_back),
+        ("k1", ("ya1", "yb1", "yf1",), core_swap),
         ("pair",),
         ("yf2", ("ya2",), y_out),
         ("ya2",),
         ("xb2", ("pair",), x_back),
-        ("k1",),
+        ("yb2",),
         ("xf2", ("xf",), z_swap),
         ("xf",),
         ("k0", ("r0", "za", "zb", "zf",), core_swap),
-        ("yb2",),
+        ("k1",),
         ("xa2", ("pair",), x_out),
         ("yf2",),
         ("k2", ("ya2", "yb2", "yf2",), core_swap),

time: 97.8 us -> 92.7 us (0.948)
  waiting for transfers between devices: 35.6 us -> 31.2 us
  starting transfers between devices: 36.8 us -> 35.3 us
    ppermute x19, waiting for transfers between devices: 35.6 us -> 31.2 us  [send(): return lax.ppermute(value, AXES, pairs)]
    ppermute x19, starting transfers between devices: 36.8 us -> 35.3 us  [send(): return lax.ppermute(value, AXES, pairs)]
  transfers between devices with their start and end apart: 19 -> 19, of which waited for: 9 -> 10; matrix products, arithmetic and copies ran while one was open for 3% -> 3% of each run, Pallas kernels for 12% -> 12%
where the time goes in v3:
time: 92.7 us; the launch traced here: 92.6 us
  starting transfers between devices  35.3 us (38%)
  waiting for transfers between devices  31.2 us (34%)
  Pallas kernels  19.7 us (21%)
  other arithmetic  3.14 us (3%)
  local copies, waits for them, and re-layouts  2.87 us (3%)
    ppermute x19, starting transfers between devices, send(): return lax.ppermute(value, AXES, pairs)  35.3 us
    ppermute x19, waiting for transfers between devices, send(): return lax.ppermute(value, AXES, pairs)  31.2 us
    pallas_call x1, Pallas kernels, body(): pl.pallas_call(functools.partial(early_kernel, len(pieces), len(early), s...  11.5 us
    pallas_call x1, Pallas kernels, body(): pl.pallas_call(functools.partial(late_kernel, len(late), scale), out_shap...  6.15 us
    unnamed x38, local copies, waits for them, and re-layouts  2.75 us
    pallas_call x1, Pallas kernels, form_rows(): pl.pallas_call(rows_kernel, out_shape=jax.ShapeDtypeStruct((1, units, tok...  2.01 us
    convert_element_type x1, other arithmetic, silu_product(): (jax.nn.silu(gate.astype(jnp.float32)) * up.astype(jnp.float32)).astype(j...  1.86 us
  transfers between devices with their start and end apart: 19, of which 10 were waited for; matrix products, arithmetic and copies ran while one was open for 3% of the time, Pallas kernels for 12%

profile of v3, /device:TPU:1, one launch (start us, length us, event | category | flops | bytes accessed | tf_op | source)
XLA Modules:
  0.0 92.6 jit_solution(259526967882419891)
XLA Ops:
  0.0 0.1 stack.163
  0.1 2.0 %shard_map.55.refs_0_ = bf16[1,1024,128]{2,1,0:T(8,128)(2,1)} custom-call(bf16[128,1024]{1,0:T(8,128)(2,1)} %gate.1, bf16[128,1024]{1,0:T(8,128)(2,1)} %up.1), custom_call_target="tpu_custom_call" | custom-call | flops 1048576 | bytes 786432 | tf_op jit(solution)/shard_map/pallas_call | solution.py:85
  2.1 6.8 %collective-permute-start = (bf16[1,1024,128]{2,1,0:T(8,128)(2,1)}, bf16[1,1024,128]{2,1,0:T(8,128)(2,1)S(1)}, u32[]{:S(2)}, u32[]{:S(2)}) collective-permute-start(bf16[1,1024,128]{2,1,0:T(8,128)(2,1)} %shard_map.55.refs_0_), channel_id=1, source_target_pairs={{0,8},{1,25},{128,136},{129,153},{8,16},{9,1},{136,144},{137,129},... | collective-permute-start | bytes 786440 | tf_op jit(solution)/shard_map/ppermute | solution.py:31
  9.0 2.7 %collective-permute-start.1 = (bf16[1,1024,128]{2,1,0:T(8,128)(2,1)}, bf16[1,1024,128]{2,1,0:T(8,128)(2,1)S(1)}, u32[]{:S(2)}, u32[]{:S(2)}) collective-permute-start(bf16[1,1024,128]{2,1,0:T(8,128)(2,1)} %shard_map.55.refs_0_), channel_id=1, source_target_pairs={{0,2},{1,7},{128,130},{129,135},{8,10},{9,15},{136,138},{137,143},... | collective-permute-start | bytes 786440 | tf_op jit(solution)/shard_map/ppermute | solution.py:31
  11.7 0.0 collective-permute-start.2
  11.7 0.0 collective-permute-start.3
  11.7 1.9 %fusion.4.refs_13_ = bf16[512,768]{1,0:T(8,128)(2,1)S(1)} fusion(bf16[512,768]{1,0:T(8,128)(2,1)} %param.9, bf16[512,768]{1,0:T(8,128)(2,1)} %param.8), kind=kLoop, calls=%fused_computation.7 | loop fusion | flops 3145728 | bytes 2359296 | tf_op jit(solution)/shard_map/convert_element_type | solution.py:74
  13.6 0.0 copy-start.6
  13.6 1.3 %collective-permute-start.4 = (bf16[512,768]{1,0:T(8,128)(2,1)S(1)}, bf16[512,768]{1,0:T(8,128)(2,1)S(1)}, u32[]{:S(2)}, u32[]{:S(2)}) collective-permute-start(bf16[512,768]{1,0:T(8,128)(2,1)S(1)} %fusion.4.refs_13_), channel_id=1, source_target_pairs={{0,96},{1,33},{128,224},{129,161},{8,104},{9,41},{136,232},{137,16... | collective-permute-start | bytes 2359304 | tf_op jit(solution)/shard_map/ppermute | solution.py:31
  14.9 4.1 %collective-permute-done.refs_1_ = bf16[1,1024,128]{2,1,0:T(8,128)(2,1)S(1)} collective-permute-done((bf16[1,1024,128]{2,1,0:T(8,128)(2,1)}, bf16[1,1024,128]{2,1,0:T(8,128)(2,1)S(1)}, u32[]{:S(2)}, u32[]{:S(2)}) %collective-permute-start) | collective-permute-done | bytes 262176 | tf_op jit(solution)/shard_map/ppermute | solution.py:31
  19.0 0.0 collective-permute-done.1.refs_2_
  19.1 0.0 collective-permute-done.2.refs_3_
  19.1 0.0 copy-start.10
  19.1 4.4 %collective-permute-start.5 = (bf16[1,1024,128]{2,1,0:T(8,128)(2,1)S(1)}, bf16[1,1024,128]{2,1,0:T(8,128)(2,1)S(1)}, u32[]{:S(2)}, u32[]{:S(2)}) collective-permute-start(bf16[1,1024,128]{2,1,0:T(8,128)(2,1)S(1)} %collective-permute-done.refs_1_), channel_id=1, source_target_pairs={{0,8},{1,25},{128,136},{129,153},{8,16},{9,1},{136,144},{137,129},... | collective-permute-start | bytes 786440 | tf_op jit(solution)/shard_map/ppermute | solution.py:31
  23.5 0.0 collective-permute-done.3.refs_4_
  23.5 2.6 %collective-permute-start.6 = (bf16[1,1024,128]{2,1,0:T(8,128)(2,1)S(1)}, bf16[1,1024,128]{2,1,0:T(8,128)(2,1)S(1)}, u32[]{:S(2)}, u32[]{:S(2)}) collective-permute-start(bf16[1,1024,128]{2,1,0:T(8,128)(2,1)S(1)} %collective-permute-done.1.refs_2_), channel_id=1, source_target_pairs={{0,2},{1,7},{128,130},{129,135},{8,10},{9,15},{136,138},{137,143},... | collective-permute-start | bytes 786440 | tf_op jit(solution)/shard_map/ppermute | solution.py:31
  26.1 2.5 %collective-permute-start.7 = (bf16[512,768]{1,0:T(8,128)(2,1)S(1)}, bf16[512,768]{1,0:T(8,128)(2,1)S(1)}, u32[]{:S(2)}, u32[]{:S(2)}) collective-permute-start(bf16[512,768]{1,0:T(8,128)(2,1)S(1)} %fusion.4.refs_13_), channel_id=1, source_target_pairs={{0,32},{1,97},{128,160},{129,225},{8,40},{9,105},{136,168},{137,23... | collective-permute-start | bytes 2359304 | tf_op jit(solution)/shard_map/ppermute | solution.py:31
  28.6 0.0 collective-permute-start.8
  28.6 0.0 collective-permute-done.5.refs_5_
  28.6 0.0 copy-start.2
  28.6 0.1 pad_maximum_fusion.2
  28.7 0.0 collective-permute-done.4.refs_16_
  28.7 0.0 copy-start.13
  28.7 0.1 pad_maximum_fusion.4
  28.8 0.2 collective-permute-start.9
  29.0 0.4 collective-permute-done.6.refs_6_
  29.4 1.0 %collective-permute-start.10 = (bf16[3,1024,128]{2,1,0:T(8,128)(2,1)S(1)}, bf16[3,1024,128]{2,1,0:T(8,128)(2,1)S(1)}, u32[]{:S(2)}, u32[]{:S(2)}) collective-permute-start(bf16[3,1024,128]{2,1,0:T(8,128)(2,1)S(1)} %pad_maximum_fusion.4), channel_id=1, source_target_pairs={{0,6},{1,3},{128,134},{129,131},{8,14},{9,11},{136,142},{137,139},... | collective-permute-start | bytes 2359304 | tf_op jit(solution)/shard_map/ppermute | solution.py:31
  30.4 0.1 pad_maximum_fusion.5
  30.5 0.0 copy-done.6
  30.5 0.0 copy-done
  30.5 0.0 copy-done.9
  30.6 0.0 copy-done.10
  30.6 0.0 copy-done.1
  30.6 0.0 copy-done.2
  30.6 0.1 pad_maximum_fusion.1
  30.7 6.7 %collective-permute-done.7.refs_15_ = bf16[512,768]{1,0:T(8,128)(2,1)S(1)} collective-permute-done((bf16[512,768]{1,0:T(8,128)(2,1)S(1)}, bf16[512,768]{1,0:T(8,128)(2,1)S(1)}, u32[]{:S(2)}, u32[]{:S(2)}) %collective-permute-start.7) | collective-permute-done | bytes 786464 | tf_op jit(solution)/shard_map/ppermute | solution.py:31
  37.5 3.4 %collective-permute-start.11 = (bf16[512,768]{1,0:T(8,128)(2,1)S(1)}, bf16[512,768]{1,0:T(8,128)(2,1)S(1)}, u32[]{:S(2)}, u32[]{:S(2)}) collective-permute-start(bf16[512,768]{1,0:T(8,128)(2,1)S(1)} %collective-permute-done.7.refs_15_), channel_id=1, source_target_pairs={{0,32},{1,97},{128,160},{129,225},{8,40},{9,105},{136,168},{137,23... | collective-permute-start | bytes 2359304 | tf_op jit(solution)/shard_map/ppermute | solution.py:31
  40.9 6.1 %collective-permute-done.8.refs_14_ = bf16[512,768]{1,0:T(8,128)(2,1)S(1)} collective-permute-done((bf16[512,768]{1,0:T(8,128)(2,1)S(1)}, bf16[512,768]{1,0:T(8,128)(2,1)S(1)}, u32[]{:S(2)}, u32[]{:S(2)}) %collective-permute-start.8) | collective-permute-done | bytes 786464 | tf_op jit(solution)/shard_map/ppermute | solution.py:31
  47.0 0.0 collective-permute-start.12
  47.0 0.0 collective-permute-done.9.refs_7_
  47.0 0.0 copy-start.3
  47.1 1.7 %collective-permute-start.13 = (bf16[3,1024,128]{2,1,0:T(8,128)(2,1)S(1)}, bf16[3,1024,128]{2,1,0:T(8,128)(2,1)S(1)}, u32[]{:S(2)}, u32[]{:S(2)}) collective-permute-start(bf16[3,1024,128]{2,1,0:T(8,128)(2,1)S(1)} %collective-permute-done.9.refs_7_), channel_id=1, source_target_pairs={{0,2},{1,7},{128,130},{129,135},{8,10},{9,15},{136,138},{137,143},... | collective-permute-start | bytes 2359304 | tf_op jit(solution)/shard_map/ppermute | solution.py:31
  48.7 0.9 collective-permute-done.10.refs_8_
  49.6 0.3 collective-permute-done.11.refs_17_
  49.9 0.0 collective-permute-done.12.refs_9_
  49.9 0.9 copy-done.17
  50.8 7.9 %collective-permute-done.13.refs_10_ = bf16[3,1024,128]{2,1,0:T(8,128)(2,1)S(1)} collective-permute-done((bf16[3,1024,128]{2,1,0:T(8,128)(2,1)S(1)}, bf16[3,1024,128]{2,1,0:T(8,128)(2,1)S(1)}, u32[]{:S(2)}, u32[]{:S(2)}) %collective-permute-start.13) | collective-permute-done | bytes 786464 | tf_op jit(solution)/shard_map/ppermute | solution.py:31
  58.7 0.3 pad_maximum_fusion
  59.0 5.9 %collective-permute-start.15 = (bf16[9,1024,128]{2,1,0:T(8,128)(2,1)S(1)}, bf16[9,1024,128]{2,1,0:T(8,128)(2,1)S(1)}, u32[]{:S(2)}, u32[]{:S(2)}) collective-permute-start(bf16[9,1024,128]{2,1,0:T(8,128)(2,1)S(1)} %pad_maximum_fusion), channel_id=1, source_target_pairs={{0,1},{1,0},{128,129},{129,128},{8,9},{9,8},{136,137},{137,136},{1... | collective-permute-start | bytes 7077896 | tf_op jit(solution)/shard_map/ppermute | solution.py:31
  64.9 0.1 collective-permute-start.14
  65.0 1.2 %collective-permute-start.17 = (bf16[512,768]{1,0:T(8,128)(2,1)S(1)}, bf16[512,768]{1,0:T(8,128)(2,1)S(1)}, u32[]{:S(2)}, u32[]{:S(2)}) collective-permute-start(bf16[512,768]{1,0:T(8,128)(2,1)S(1)} %collective-permute-done.8.refs_14_), channel_id=1, source_target_pairs={{0,96},{1,33},{128,224},{129,161},{8,104},{9,41},{136,232},{137,16... | collective-permute-start | bytes 2359304 | tf_op jit(solution)/shard_map/ppermute | solution.py:31
  66.2 1.5 %collective-permute-start.16 = (bf16[512,768]{1,0:T(8,128)(2,1)S(1)}, bf16[512,768]{1,0:T(8,128)(2,1)}, u32[]{:S(2)}, u32[]{:S(2)}) collective-permute-start(bf16[512,768]{1,0:T(8,128)(2,1)S(1)} %collective-permute-done.8.refs_14_), channel_id=1, source_target_pairs={{0,32},{1,97},{128,160},{129,225},{8,40},{9,105},{136,168},{137,23... | collective-permute-start | bytes 2359304 | tf_op jit(solution)/shard_map/ppermute | solution.py:31
  67.7 0.0 collective-permute-start.18
  67.7 2.9 %collective-permute-done.14.refs_11_ = bf16[4,1024,128]{2,1,0:T(8,128)(2,1)S(1)} collective-permute-done((bf16[4,1024,128]{2,1,0:T(8,128)(2,1)S(1)}, bf16[4,1024,128]{2,1,0:T(8,128)(2,1)S(1)}, u32[]{:S(2)}, u32[]{:S(2)}) %collective-permute-start.14) | collective-permute-done | bytes 1048608 | tf_op jit(solution)/shard_map/ppermute | solution.py:31
  70.6 0.6 broadcast_add_fusion.table
  71.1 0.0 collective-permute-done.15.refs_12_
  71.1 0.4 copy-done.12
  71.5 1.4 %copy-done.8 = bf16[9,1024,128]{2,1,0:T(8,128)(2,1)} copy-done((bf16[9,1024,128]{2,1,0:T(8,128)(2,1)}, bf16[9,1024,128]{2,1,0:T(8,128)(2,1)S(1)}, u32[]{:S(2)}) %copy-start.8) | copy-done | bytes 2359320
  72.9 11.5 %shard_map.56 = (f32[1024,768]{1,0:T(8,128)}, bf16[12,1024,128]{2,1,0:T(8,128)(2,1)}) custom-call(s32[40]{0:T(128)} %broadcast_add_fusion.table, f32[1024,768]{1,0:T(8,128)} %hessian.1, bf16[1,1024,128]{2,1,0:T(8,128)(2,1)} %shard_map.55.refs_0_, bf16[1,1024,128]{2,1,0:T(8,128)(2,1)} %copy-done, bf16[1,1024,128]{2,1,0:T(8,128)(2,1)} %copy-done.9, ...), custom_call_target="tpu_custom_call" | custom-call | flops 4026531840 | bytes 15466496 | tf_op jit(solution)/shard_map/pallas_call | solution.py:278
  84.4 0.0 collective-permute-done.17.refs_1_
  84.4 0.0 copy-start.18
  84.5 1.1 %collective-permute-done.16.refs_0_ = bf16[512,768]{1,0:T(8,128)(2,1)} collective-permute-done((bf16[512,768]{1,0:T(8,128)(2,1)S(1)}, bf16[512,768]{1,0:T(8,128)(2,1)}, u32[]{:S(2)}, u32[]{:S(2)}) %collective-permute-start.16) | collective-permute-done | bytes 786464 | tf_op jit(solution)/shard_map/ppermute | solution.py:31
  85.5 0.8 collective-permute-done.18.refs_2_
  86.3 6.2 %shard_map.57 = f32[1024,768]{1,0:T(8,128)} custom-call(f32[1024,768]{1,0:T(8,128)} %get-tuple-element.148.partial, bf16[12,1024,128]{2,1,0:T(8,128)(2,1)} %get-tuple-element.149.late_rows, bf16[512,768]{1,0:T(8,128)(2,1)} %collective-permute-done.16.refs_0_, bf16[512,768]{1,0:T(8,128)(2,1)} %copy-done.18, bf16[512,768]{1,0:T(8,128)(2,1)} %collective-permute-done.18.refs_2_), custom_call_target="tpu_custom_call" | custom-call | flops 2415919104 | bytes 11796480 | tf_op jit(solution)/shard_map/pallas_call | solution.py:298
  (39 shorter events, 0.1 us)
Async XLA Ops:
  2.1 16.9 %collective-permute-start = (bf16[1,1024,128]{2,1,0:T(8,128)(2,1)}, bf16[1,1024,128]{2,1,0:T(8,128)(2,1)S(1)}, u32[]{:S(2)}, u32[]{:S(2)}) collective-permute-start(bf16[1,1024,128]{2,1,0:T(8,128)(2,1)} %shard_map.55.refs_0_), channel_id=1, source_target_pairs={{0,8},{1,25},{128,136},{129,153},{8,16},{9,1},{136,144},{137,129},... | collective-permute-start | bytes 786440 | tf_op jit(solution)/shard_map/ppermute | solution.py:31
  9.0 10.0 %collective-permute-start.1 = (bf16[1,1024,128]{2,1,0:T(8,128)(2,1)}, bf16[1,1024,128]{2,1,0:T(8,128)(2,1)S(1)}, u32[]{:S(2)}, u32[]{:S(2)}) collective-permute-start(bf16[1,1024,128]{2,1,0:T(8,128)(2,1)} %shard_map.55.refs_0_), channel_id=1, source_target_pairs={{0,2},{1,7},{128,130},{129,135},{8,10},{9,15},{136,138},{137,143},... | collective-permute-start | bytes 786440 | tf_op jit(solution)/shard_map/ppermute | solution.py:31
  11.7 7.3 %collective-permute-start.2 = (bf16[1,1024,128]{2,1,0:T(8,128)(2,1)}, bf16[1,1024,128]{2,1,0:T(8,128)(2,1)S(1)}, u32[]{:S(2)}, u32[]{:S(2)}) collective-permute-start(bf16[1,1024,128]{2,1,0:T(8,128)(2,1)} %shard_map.55.refs_0_), channel_id=1, source_target_pairs={{0,6},{1,3},{128,134},{129,131},{8,14},{9,11},{136,142},{137,139},... | collective-permute-start | bytes 786440 | tf_op jit(solution)/shard_map/ppermute | solution.py:31
  11.7 11.8 %collective-permute-start.3 = (bf16[1,1024,128]{2,1,0:T(8,128)(2,1)}, bf16[1,1024,128]{2,1,0:T(8,128)(2,1)S(1)}, u32[]{:S(2)}, u32[]{:S(2)}) collective-permute-start(bf16[1,1024,128]{2,1,0:T(8,128)(2,1)} %shard_map.55.refs_0_), channel_id=1, source_target_pairs={{0,24},{1,9},{128,152},{129,137},{8,0},{9,17},{136,128},{137,145},... | collective-permute-start | bytes 786440 | tf_op jit(solution)/shard_map/ppermute | solution.py:31
  13.6 16.9 %copy-start.6 = (bf16[512,768]{1,0:T(8,128)(2,1)}, bf16[512,768]{1,0:T(8,128)(2,1)S(1)}, u32[]{:S(2)}) copy-start(bf16[512,768]{1,0:T(8,128)(2,1)S(1)} %fusion.4.refs_13_) | copy-start | bytes 2359300
  13.6 15.1 %collective-permute-start.4 = (bf16[512,768]{1,0:T(8,128)(2,1)S(1)}, bf16[512,768]{1,0:T(8,128)(2,1)S(1)}, u32[]{:S(2)}, u32[]{:S(2)}) collective-permute-start(bf16[512,768]{1,0:T(8,128)(2,1)S(1)} %fusion.4.refs_13_), channel_id=1, source_target_pairs={{0,96},{1,33},{128,224},{129,161},{8,104},{9,41},{136,232},{137,16... | collective-permute-start | bytes 2359304 | tf_op jit(solution)/shard_map/ppermute | solution.py:31
  19.0 11.5 %copy-start = (bf16[1,1024,128]{2,1,0:T(8,128)(2,1)}, bf16[1,1024,128]{2,1,0:T(8,128)(2,1)S(1)}, u32[]{:S(2)}) copy-start(bf16[1,1024,128]{2,1,0:T(8,128)(2,1)S(1)} %collective-permute-done.refs_1_) | copy-start | bytes 786436
  19.0 11.5 %copy-start.9 = (bf16[1,1024,128]{2,1,0:T(8,128)(2,1)}, bf16[1,1024,128]{2,1,0:T(8,128)(2,1)S(1)}, u32[]{:S(2)}) copy-start(bf16[1,1024,128]{2,1,0:T(8,128)(2,1)S(1)} %collective-permute-done.1.refs_2_) | copy-start | bytes 786436
  19.1 11.5 %copy-start.10 = (bf16[1,1024,128]{2,1,0:T(8,128)(2,1)}, bf16[1,1024,128]{2,1,0:T(8,128)(2,1)S(1)}, u32[]{:S(2)}) copy-start(bf16[1,1024,128]{2,1,0:T(8,128)(2,1)S(1)} %collective-permute-done.2.refs_3_) | copy-start | bytes 786436
  19.1 9.5 %collective-permute-start.5 = (bf16[1,1024,128]{2,1,0:T(8,128)(2,1)S(1)}, bf16[1,1024,128]{2,1,0:T(8,128)(2,1)S(1)}, u32[]{:S(2)}, u32[]{:S(2)}) collective-permute-start(bf16[1,1024,128]{2,1,0:T(8,128)(2,1)S(1)} %collective-permute-done.refs_1_), channel_id=1, source_target_pairs={{0,8},{1,25},{128,136},{129,153},{8,16},{9,1},{136,144},{137,129},... | collective-permute-start | bytes 786440 | tf_op jit(solution)/shard_map/ppermute | solution.py:31
  23.5 7.0 %copy-start.1 = (bf16[1,1024,128]{2,1,0:T(8,128)(2,1)}, bf16[1,1024,128]{2,1,0:T(8,128)(2,1)S(1)}, u32[]{:S(2)}) copy-start(bf16[1,1024,128]{2,1,0:T(8,128)(2,1)S(1)} %collective-permute-done.3.refs_4_) | copy-start | bytes 786436
  23.5 5.9 %collective-permute-start.6 = (bf16[1,1024,128]{2,1,0:T(8,128)(2,1)S(1)}, bf16[1,1024,128]{2,1,0:T(8,128)(2,1)S(1)}, u32[]{:S(2)}, u32[]{:S(2)}) collective-permute-start(bf16[1,1024,128]{2,1,0:T(8,128)(2,1)S(1)} %collective-permute-done.1.refs_2_), channel_id=1, source_target_pairs={{0,2},{1,7},{128,130},{129,135},{8,10},{9,15},{136,138},{137,143},... | collective-permute-start | bytes 786440 | tf_op jit(solution)/shard_map/ppermute | solution.py:31
  26.1 11.4 %collective-permute-start.7 = (bf16[512,768]{1,0:T(8,128)(2,1)S(1)}, bf16[512,768]{1,0:T(8,128)(2,1)S(1)}, u32[]{:S(2)}, u32[]{:S(2)}) collective-permute-start(bf16[512,768]{1,0:T(8,128)(2,1)S(1)} %fusion.4.refs_13_), channel_id=1, source_target_pairs={{0,32},{1,97},{128,160},{129,225},{8,40},{9,105},{136,168},{137,23... | collective-permute-start | bytes 2359304 | tf_op jit(solution)/shard_map/ppermute | solution.py:31
  28.6 18.5 %collective-permute-start.8 = (bf16[512,768]{1,0:T(8,128)(2,1)S(1)}, bf16[512,768]{1,0:T(8,128)(2,1)S(1)}, u32[]{:S(2)}, u32[]{:S(2)}) collective-permute-start(bf16[512,768]{1,0:T(8,128)(2,1)S(1)} %fusion.4.refs_13_), channel_id=1, source_target_pairs={{0,128},{1,129},{128,0},{129,1},{8,136},{9,137},{136,8},{137,9},{1... | collective-permute-start | bytes 2359304 | tf_op jit(solution)/shard_map/ppermute | solution.py:31
  28.6 2.0 %copy-start.7 = (bf16[1,1024,128]{2,1,0:T(8,128)(2,1)S(1)}, bf16[1,1024,128]{2,1,0:T(8,128)(2,1)}, u32[]{:S(2)}) copy-start(bf16[1,1024,128]{2,1,0:T(8,128)(2,1)} %shard_map.55.refs_0_) | copy-start | bytes 786436
  28.6 2.0 %copy-start.2 = (bf16[1,1024,128]{2,1,0:T(8,128)(2,1)}, bf16[1,1024,128]{2,1,0:T(8,128)(2,1)S(1)}, u32[]{:S(2)}) copy-start(bf16[1,1024,128]{2,1,0:T(8,128)(2,1)S(1)} %collective-permute-done.5.refs_5_) | copy-start | bytes 786436
  28.7 2.0 %copy-start.13 = (bf16[512,768]{1,0:T(8,128)(2,1)}, bf16[512,768]{1,0:T(8,128)(2,1)S(1)}, u32[]{:S(2)}) copy-start(bf16[512,768]{1,0:T(8,128)(2,1)S(1)} %collective-permute-done.4.refs_16_) | copy-start | bytes 2359300
  28.8 18.2 %collective-permute-start.9 = (bf16[3,1024,128]{2,1,0:T(8,128)(2,1)S(1)}, bf16[3,1024,128]{2,1,0:T(8,128)(2,1)S(1)}, u32[]{:S(2)}, u32[]{:S(2)}) collective-permute-start(bf16[3,1024,128]{2,1,0:T(8,128)(2,1)S(1)} %pad_maximum_fusion.2), channel_id=1, source_target_pairs={{0,2},{1,7},{128,130},{129,135},{8,10},{9,15},{136,138},{137,143},... | collective-permute-start | bytes 2359304 | tf_op jit(solution)/shard_map/ppermute | solution.py:31
  29.4 29.5 %copy-start.11 = (bf16[1,1024,128]{2,1,0:T(8,128)(2,1)}, bf16[1,1024,128]{2,1,0:T(8,128)(2,1)S(1)}, u32[]{:S(2)}) copy-start(bf16[1,1024,128]{2,1,0:T(8,128)(2,1)S(1)} %collective-permute-done.6.refs_6_) | copy-start | bytes 786436
  29.4 20.2 %collective-permute-start.10 = (bf16[3,1024,128]{2,1,0:T(8,128)(2,1)S(1)}, bf16[3,1024,128]{2,1,0:T(8,128)(2,1)S(1)}, u32[]{:S(2)}, u32[]{:S(2)}) collective-permute-start(bf16[3,1024,128]{2,1,0:T(8,128)(2,1)S(1)} %pad_maximum_fusion.4), channel_id=1, source_target_pairs={{0,6},{1,3},{128,134},{129,131},{8,14},{9,11},{136,142},{137,139},... | collective-permute-start | bytes 2359304 | tf_op jit(solution)/shard_map/ppermute | solution.py:31
  37.5 21.5 %copy-start.15 = (bf16[512,768]{1,0:T(8,128)(2,1)}, bf16[512,768]{1,0:T(8,128)(2,1)S(1)}, u32[]{:S(2)}) copy-start(bf16[512,768]{1,0:T(8,128)(2,1)S(1)} %collective-permute-done.7.refs_15_) | copy-start | bytes 2359300
  37.5 12.3 %collective-permute-start.11 = (bf16[512,768]{1,0:T(8,128)(2,1)S(1)}, bf16[512,768]{1,0:T(8,128)(2,1)S(1)}, u32[]{:S(2)}, u32[]{:S(2)}) collective-permute-start(bf16[512,768]{1,0:T(8,128)(2,1)S(1)} %collective-permute-done.7.refs_15_), channel_id=1, source_target_pairs={{0,32},{1,97},{128,160},{129,225},{8,40},{9,105},{136,168},{137,23... | collective-permute-start | bytes 2359304 | tf_op jit(solution)/shard_map/ppermute | solution.py:31
  47.0 19.2 %copy-start.14 = (bf16[512,768]{1,0:T(8,128)(2,1)}, bf16[512,768]{1,0:T(8,128)(2,1)S(1)}, u32[]{:S(2)}) copy-start(bf16[512,768]{1,0:T(8,128)(2,1)S(1)} %collective-permute-done.8.refs_14_) | copy-start | bytes 2359300
  47.0 2.8 %collective-permute-start.12 = (bf16[3,1024,128]{2,1,0:T(8,128)(2,1)S(1)}, bf16[3,1024,128]{2,1,0:T(8,128)(2,1)S(1)}, u32[]{:S(2)}, u32[]{:S(2)}) collective-permute-start(bf16[3,1024,128]{2,1,0:T(8,128)(2,1)S(1)} %pad_maximum_fusion.5), channel_id=1, source_target_pairs={{0,1},{1,0},{128,129},{129,128},{8,9},{9,8},{136,137},{137,136},{1... | collective-permute-start | bytes 2359304 | tf_op jit(solution)/shard_map/ppermute | solution.py:31
  47.0 11.9 %copy-start.3 = (bf16[3,1024,128]{2,1,0:T(8,128)(2,1)}, bf16[3,1024,128]{2,1,0:T(8,128)(2,1)S(1)}, u32[]{:S(2)}) copy-start(bf16[3,1024,128]{2,1,0:T(8,128)(2,1)S(1)} %collective-permute-done.9.refs_7_) | copy-start | bytes 2359300
  47.1 11.6 %collective-permute-start.13 = (bf16[3,1024,128]{2,1,0:T(8,128)(2,1)S(1)}, bf16[3,1024,128]{2,1,0:T(8,128)(2,1)S(1)}, u32[]{:S(2)}, u32[]{:S(2)}) collective-permute-start(bf16[3,1024,128]{2,1,0:T(8,128)(2,1)S(1)} %collective-permute-done.9.refs_7_), channel_id=1, source_target_pairs={{0,2},{1,7},{128,130},{129,135},{8,10},{9,15},{136,138},{137,143},... | collective-permute-start | bytes 2359304 | tf_op jit(solution)/shard_map/ppermute | solution.py:31
  49.6 9.4 %copy-start.4 = (bf16[3,1024,128]{2,1,0:T(8,128)(2,1)}, bf16[3,1024,128]{2,1,0:T(8,128)(2,1)S(1)}, u32[]{:S(2)}) copy-start(bf16[3,1024,128]{2,1,0:T(8,128)(2,1)S(1)} %collective-permute-done.10.refs_8_) | copy-start | bytes 2359300
  49.8 17.8 %copy-start.16 = (bf16[512,768]{1,0:T(8,128)(2,1)}, bf16[512,768]{1,0:T(8,128)(2,1)S(1)}, u32[]{:S(2)}) copy-start(bf16[512,768]{1,0:T(8,128)(2,1)S(1)} %collective-permute-done.11.refs_17_) | copy-start | bytes 2359300
  49.9 0.9 copy-start.17
  58.7 9.0 %copy-start.5 = (bf16[3,1024,128]{2,1,0:T(8,128)(2,1)}, bf16[3,1024,128]{2,1,0:T(8,128)(2,1)S(1)}, u32[]{:S(2)}) copy-start(bf16[3,1024,128]{2,1,0:T(8,128)(2,1)S(1)} %collective-permute-done.13.refs_10_) | copy-start | bytes 2359300
  59.0 12.2 %collective-permute-start.15 = (bf16[9,1024,128]{2,1,0:T(8,128)(2,1)S(1)}, bf16[9,1024,128]{2,1,0:T(8,128)(2,1)S(1)}, u32[]{:S(2)}, u32[]{:S(2)}) collective-permute-start(bf16[9,1024,128]{2,1,0:T(8,128)(2,1)S(1)} %pad_maximum_fusion), channel_id=1, source_target_pairs={{0,1},{1,0},{128,129},{129,128},{8,9},{9,8},{136,137},{137,136},{1... | collective-permute-start | bytes 7077896 | tf_op jit(solution)/shard_map/ppermute | solution.py:31
  64.9 5.7 %collective-permute-start.14 = (bf16[4,1024,128]{2,1,0:T(8,128)(2,1)S(1)}, bf16[4,1024,128]{2,1,0:T(8,128)(2,1)S(1)}, u32[]{:S(2)}, u32[]{:S(2)}) collective-permute-start(bf16[4,1024,128]{2,1,0:T(8,128)(2,1)S(1)} %pad_maximum_fusion.1), channel_id=1, source_target_pairs={{0,1},{1,0},{128,129},{129,128},{8,9},{9,8},{136,137},{137,136},{1... | collective-permute-start | bytes 3145736 | tf_op jit(solution)/shard_map/ppermute | solution.py:31
  65.0 19.4 %collective-permute-start.17 = (bf16[512,768]{1,0:T(8,128)(2,1)S(1)}, bf16[512,768]{1,0:T(8,128)(2,1)S(1)}, u32[]{:S(2)}, u32[]{:S(2)}) collective-permute-start(bf16[512,768]{1,0:T(8,128)(2,1)S(1)} %collective-permute-done.8.refs_14_), channel_id=1, source_target_pairs={{0,96},{1,33},{128,224},{129,161},{8,104},{9,41},{136,232},{137,16... | collective-permute-start | bytes 2359304 | tf_op jit(solution)/shard_map/ppermute | solution.py:31
  66.2 19.3 %collective-permute-start.16 = (bf16[512,768]{1,0:T(8,128)(2,1)S(1)}, bf16[512,768]{1,0:T(8,128)(2,1)}, u32[]{:S(2)}, u32[]{:S(2)}) collective-permute-start(bf16[512,768]{1,0:T(8,128)(2,1)S(1)} %collective-permute-done.8.refs_14_), channel_id=1, source_target_pairs={{0,32},{1,97},{128,160},{129,225},{8,40},{9,105},{136,168},{137,23... | collective-permute-start | bytes 2359304 | tf_op jit(solution)/shard_map/ppermute | solution.py:31
  67.7 18.6 %collective-permute-start.18 = (bf16[512,768]{1,0:T(8,128)(2,1)S(1)}, bf16[512,768]{1,0:T(8,128)(2,1)}, u32[]{:S(2)}, u32[]{:S(2)}) collective-permute-start(bf16[512,768]{1,0:T(8,128)(2,1)S(1)} %collective-permute-done.11.refs_17_), channel_id=1, source_target_pairs={{0,128},{1,129},{128,0},{129,1},{8,136},{9,137},{136,8},{137,9},{1... | collective-permute-start | bytes 2359304 | tf_op jit(solution)/shard_map/ppermute | solution.py:31
  70.6 1.0 %copy-start.12 = (bf16[4,1024,128]{2,1,0:T(8,128)(2,1)}, bf16[4,1024,128]{2,1,0:T(8,128)(2,1)S(1)}, u32[]{:S(2)}) copy-start(bf16[4,1024,128]{2,1,0:T(8,128)(2,1)S(1)} %collective-permute-done.14.refs_11_) | copy-start | bytes 3145732
  71.5 1.4 %copy-start.8 = (bf16[9,1024,128]{2,1,0:T(8,128)(2,1)}, bf16[9,1024,128]{2,1,0:T(8,128)(2,1)S(1)}, u32[]{:S(2)}) copy-start(bf16[9,1024,128]{2,1,0:T(8,128)(2,1)S(1)} %collective-permute-done.15.refs_12_) | copy-start | bytes 7077892
  84.4 1.9 %copy-start.18 = (bf16[512,768]{1,0:T(8,128)(2,1)}, bf16[512,768]{1,0:T(8,128)(2,1)S(1)}, u32[]{:S(2)}) copy-start(bf16[512,768]{1,0:T(8,128)(2,1)S(1)} %collective-permute-done.17.refs_1_) | copy-start | bytes 2359300

commit v4 on v3

--- a/solution.py
+++ b/solution.py
@@ -8,7 +8,7 @@
 from jax.sharding import PartitionSpec as P
 
 AXES = ("row", "col")
-CHUNK = 512
+CHUNK = 256
 VMEM = pl.BlockSpec(memory_space=pltpu.VMEM)
 SMEM = pl.BlockSpec(memory_space=pltpu.SMEM)
 HBM = pl.BlockSpec(memory_space=pltpu.HBM)

time: 92.7 us -> 92.3 us (level)
  no operation moved by 1% of the time
where the time goes in v4:
time: 92.3 us; the launch traced here: 92.2 us
  starting transfers between devices  35.3 us (38%)
  waiting for transfers between devices  31.2 us (34%)
  Pallas kernels  19.2 us (21%)
  other arithmetic  3.14 us (3%)
  local copies, waits for them, and re-layouts  2.87 us (3%)
    ppermute x19, starting transfers between devices, send(): return lax.ppermute(value, AXES, pairs)  35.3 us
    ppermute x19, waiting for transfers between devices, send(): return lax.ppermute(value, AXES, pairs)  31.2 us
    pallas_call x1, Pallas kernels, body(): pl.pallas_call(functools.partial(early_kernel, len(pieces), len(early), s...  11.4 us
    pallas_call x1, Pallas kernels, body(): pl.pallas_call(functools.partial(late_kernel, len(late), scale), out_shap...  5.73 us
    unnamed x38, local copies, waits for them, and re-layouts  2.75 us
    pallas_call x1, Pallas kernels, form_rows(): pl.pallas_call(rows_kernel, out_shape=jax.ShapeDtypeStruct((1, units, tok...  2.01 us
    convert_element_type x1, other arithmetic, silu_product(): (jax.nn.silu(gate.astype(jnp.float32)) * up.astype(jnp.float32)).astype(j...  1.86 us
  transfers between devices with their start and end apart: 19, of which 10 were waited for; matrix products, arithmetic and copies ran while one was open for 3% of the time, Pallas kernels for 12%

profile of v4, /device:TPU:1, one launch (start us, length us, event | category | flops | bytes accessed | tf_op | source)
XLA Modules:
  0.0 92.2 jit_solution(16914126051923716665)
XLA Ops:
  0.0 0.1 stack.163
  0.1 2.0 %shard_map.55.refs_0_ = bf16[1,1024,128]{2,1,0:T(8,128)(2,1)} custom-call(bf16[128,1024]{1,0:T(8,128)(2,1)} %gate.1, bf16[128,1024]{1,0:T(8,128)(2,1)} %up.1), custom_call_target="tpu_custom_call" | custom-call | flops 1048576 | bytes 786432 | tf_op jit(solution)/shard_map/pallas_call | solution.py:85
  2.1 6.8 %collective-permute-start = (bf16[1,1024,128]{2,1,0:T(8,128)(2,1)}, bf16[1,1024,128]{2,1,0:T(8,128)(2,1)S(1)}, u32[]{:S(2)}, u32[]{:S(2)}) collective-permute-start(bf16[1,1024,128]{2,1,0:T(8,128)(2,1)} %shard_map.55.refs_0_), channel_id=1, source_target_pairs={{0,8},{1,25},{128,136},{129,153},{8,16},{9,1},{136,144},{137,129},... | collective-permute-start | bytes 786440 | tf_op jit(solution)/shard_map/ppermute | solution.py:31
  9.0 2.7 %collective-permute-start.1 = (bf16[1,1024,128]{2,1,0:T(8,128)(2,1)}, bf16[1,1024,128]{2,1,0:T(8,128)(2,1)S(1)}, u32[]{:S(2)}, u32[]{:S(2)}) collective-permute-start(bf16[1,1024,128]{2,1,0:T(8,128)(2,1)} %shard_map.55.refs_0_), channel_id=1, source_target_pairs={{0,2},{1,7},{128,130},{129,135},{8,10},{9,15},{136,138},{137,143},... | collective-permute-start | bytes 786440 | tf_op jit(solution)/shard_map/ppermute | solution.py:31
  11.7 0.0 collective-permute-start.2
  11.7 0.0 collective-permute-start.3
  11.7 1.9 %fusion.4.refs_13_ = bf16[512,768]{1,0:T(8,128)(2,1)S(1)} fusion(bf16[512,768]{1,0:T(8,128)(2,1)} %param.9, bf16[512,768]{1,0:T(8,128)(2,1)} %param.8), kind=kLoop, calls=%fused_computation.7 | loop fusion | flops 3145728 | bytes 2359296 | tf_op jit(solution)/shard_map/convert_element_type | solution.py:74
  13.6 0.0 copy-start.6
  13.6 1.3 %collective-permute-start.4 = (bf16[512,768]{1,0:T(8,128)(2,1)S(1)}, bf16[512,768]{1,0:T(8,128)(2,1)S(1)}, u32[]{:S(2)}, u32[]{:S(2)}) collective-permute-start(bf16[512,768]{1,0:T(8,128)(2,1)S(1)} %fusion.4.refs_13_), channel_id=1, source_target_pairs={{0,96},{1,33},{128,224},{129,161},{8,104},{9,41},{136,232},{137,16... | collective-permute-start | bytes 2359304 | tf_op jit(solution)/shard_map/ppermute | solution.py:31
  14.9 4.1 %collective-permute-done.refs_1_ = bf16[1,1024,128]{2,1,0:T(8,128)(2,1)S(1)} collective-permute-done((bf16[1,1024,128]{2,1,0:T(8,128)(2,1)}, bf16[1,1024,128]{2,1,0:T(8,128)(2,1)S(1)}, u32[]{:S(2)}, u32[]{:S(2)}) %collective-permute-start) | collective-permute-done | bytes 262176 | tf_op jit(solution)/shard_map/ppermute | solution.py:31
  19.0 0.0 collective-permute-done.1.refs_2_
  19.1 0.0 collective-permute-done.2.refs_3_
  19.1 0.0 copy-start.10
  19.1 4.4 %collective-permute-start.5 = (bf16[1,1024,128]{2,1,0:T(8,128)(2,1)S(1)}, bf16[1,1024,128]{2,1,0:T(8,128)(2,1)S(1)}, u32[]{:S(2)}, u32[]{:S(2)}) collective-permute-start(bf16[1,1024,128]{2,1,0:T(8,128)(2,1)S(1)} %collective-permute-done.refs_1_), channel_id=1, source_target_pairs={{0,8},{1,25},{128,136},{129,153},{8,16},{9,1},{136,144},{137,129},... | collective-permute-start | bytes 786440 | tf_op jit(solution)/shard_map/ppermute | solution.py:31
  23.5 0.0 collective-permute-done.3.refs_4_
  23.5 2.6 %collective-permute-start.6 = (bf16[1,1024,128]{2,1,0:T(8,128)(2,1)S(1)}, bf16[1,1024,128]{2,1,0:T(8,128)(2,1)S(1)}, u32[]{:S(2)}, u32[]{:S(2)}) collective-permute-start(bf16[1,1024,128]{2,1,0:T(8,128)(2,1)S(1)} %collective-permute-done.1.refs_2_), channel_id=1, source_target_pairs={{0,2},{1,7},{128,130},{129,135},{8,10},{9,15},{136,138},{137,143},... | collective-permute-start | bytes 786440 | tf_op jit(solution)/shard_map/ppermute | solution.py:31
  26.1 2.5 %collective-permute-start.7 = (bf16[512,768]{1,0:T(8,128)(2,1)S(1)}, bf16[512,768]{1,0:T(8,128)(2,1)S(1)}, u32[]{:S(2)}, u32[]{:S(2)}) collective-permute-start(bf16[512,768]{1,0:T(8,128)(2,1)S(1)} %fusion.4.refs_13_), channel_id=1, source_target_pairs={{0,32},{1,97},{128,160},{129,225},{8,40},{9,105},{136,168},{137,23... | collective-permute-start | bytes 2359304 | tf_op jit(solution)/shard_map/ppermute | solution.py:31
  28.6 0.0 collective-permute-start.8
  28.6 0.0 collective-permute-done.5.refs_5_
  28.6 0.0 copy-start.2
  28.6 0.1 pad_maximum_fusion.2
  28.7 0.0 collective-permute-done.4.refs_16_
  28.7 0.0 copy-start.13
  28.7 0.1 pad_maximum_fusion.4
  28.8 0.2 collective-permute-start.9
  29.0 0.4 collective-permute-done.6.refs_6_
  29.4 1.0 %collective-permute-start.10 = (bf16[3,1024,128]{2,1,0:T(8,128)(2,1)S(1)}, bf16[3,1024,128]{2,1,0:T(8,128)(2,1)S(1)}, u32[]{:S(2)}, u32[]{:S(2)}) collective-permute-start(bf16[3,1024,128]{2,1,0:T(8,128)(2,1)S(1)} %pad_maximum_fusion.4), channel_id=1, source_target_pairs={{0,6},{1,3},{128,134},{129,131},{8,14},{9,11},{136,142},{137,139},... | collective-permute-start | bytes 2359304 | tf_op jit(solution)/shard_map/ppermute | solution.py:31
  30.4 0.1 pad_maximum_fusion.5
  30.5 0.0 copy-done.6
  30.5 0.0 copy-done
  30.5 0.0 copy-done.9
  30.6 0.0 copy-done.10
  30.6 0.0 copy-done.1
  30.6 0.0 copy-done.2
  30.6 0.1 pad_maximum_fusion.1
  30.7 6.7 %collective-permute-done.7.refs_15_ = bf16[512,768]{1,0:T(8,128)(2,1)S(1)} collective-permute-done((bf16[512,768]{1,0:T(8,128)(2,1)S(1)}, bf16[512,768]{1,0:T(8,128)(2,1)S(1)}, u32[]{:S(2)}, u32[]{:S(2)}) %collective-permute-start.7) | collective-permute-done | bytes 786464 | tf_op jit(solution)/shard_map/ppermute | solution.py:31
  37.5 3.4 %collective-permute-start.11 = (bf16[512,768]{1,0:T(8,128)(2,1)S(1)}, bf16[512,768]{1,0:T(8,128)(2,1)S(1)}, u32[]{:S(2)}, u32[]{:S(2)}) collective-permute-start(bf16[512,768]{1,0:T(8,128)(2,1)S(1)} %collective-permute-done.7.refs_15_), channel_id=1, source_target_pairs={{0,32},{1,97},{128,160},{129,225},{8,40},{9,105},{136,168},{137,23... | collective-permute-start | bytes 2359304 | tf_op jit(solution)/shard_map/ppermute | solution.py:31
  40.9 6.1 %collective-permute-done.8.refs_14_ = bf16[512,768]{1,0:T(8,128)(2,1)S(1)} collective-permute-done((bf16[512,768]{1,0:T(8,128)(2,1)S(1)}, bf16[512,768]{1,0:T(8,128)(2,1)S(1)}, u32[]{:S(2)}, u32[]{:S(2)}) %collective-permute-start.8) | collective-permute-done | bytes 786464 | tf_op jit(solution)/shard_map/ppermute | solution.py:31
  47.0 0.0 collective-permute-start.12
  47.0 0.0 collective-permute-done.9.refs_7_
  47.0 0.0 copy-start.3
  47.1 1.7 %collective-permute-start.13 = (bf16[3,1024,128]{2,1,0:T(8,128)(2,1)S(1)}, bf16[3,1024,128]{2,1,0:T(8,128)(2,1)S(1)}, u32[]{:S(2)}, u32[]{:S(2)}) collective-permute-start(bf16[3,1024,128]{2,1,0:T(8,128)(2,1)S(1)} %collective-permute-done.9.refs_7_), channel_id=1, source_target_pairs={{0,2},{1,7},{128,130},{129,135},{8,10},{9,15},{136,138},{137,143},... | collective-permute-start | bytes 2359304 | tf_op jit(solution)/shard_map/ppermute | solution.py:31
  48.7 0.9 collective-permute-done.10.refs_8_
  49.6 0.3 collective-permute-done.11.refs_17_
  49.9 0.0 collective-permute-done.12.refs_9_
  49.9 0.9 copy-done.17
  50.8 7.9 %collective-permute-done.13.refs_10_ = bf16[3,1024,128]{2,1,0:T(8,128)(2,1)S(1)} collective-permute-done((bf16[3,1024,128]{2,1,0:T(8,128)(2,1)S(1)}, bf16[3,1024,128]{2,1,0:T(8,128)(2,1)S(1)}, u32[]{:S(2)}, u32[]{:S(2)}) %collective-permute-start.13) | collective-permute-done | bytes 786464 | tf_op jit(solution)/shard_map/ppermute | solution.py:31
  58.7 0.3 pad_maximum_fusion
  59.0 5.9 %collective-permute-start.15 = (bf16[9,1024,128]{2,1,0:T(8,128)(2,1)S(1)}, bf16[9,1024,128]{2,1,0:T(8,128)(2,1)S(1)}, u32[]{:S(2)}, u32[]{:S(2)}) collective-permute-start(bf16[9,1024,128]{2,1,0:T(8,128)(2,1)S(1)} %pad_maximum_fusion), channel_id=1, source_target_pairs={{0,1},{1,0},{128,129},{129,128},{8,9},{9,8},{136,137},{137,136},{1... | collective-permute-start | bytes 7077896 | tf_op jit(solution)/shard_map/ppermute | solution.py:31
  64.9 0.1 collective-permute-start.14
  65.0 1.2 %collective-permute-start.17 = (bf16[512,768]{1,0:T(8,128)(2,1)S(1)}, bf16[512,768]{1,0:T(8,128)(2,1)S(1)}, u32[]{:S(2)}, u32[]{:S(2)}) collective-permute-start(bf16[512,768]{1,0:T(8,128)(2,1)S(1)} %collective-permute-done.8.refs_14_), channel_id=1, source_target_pairs={{0,96},{1,33},{128,224},{129,161},{8,104},{9,41},{136,232},{137,16... | collective-permute-start | bytes 2359304 | tf_op jit(solution)/shard_map/ppermute | solution.py:31
  66.2 1.5 %collective-permute-start.16 = (bf16[512,768]{1,0:T(8,128)(2,1)S(1)}, bf16[512,768]{1,0:T(8,128)(2,1)}, u32[]{:S(2)}, u32[]{:S(2)}) collective-permute-start(bf16[512,768]{1,0:T(8,128)(2,1)S(1)} %collective-permute-done.8.refs_14_), channel_id=1, source_target_pairs={{0,32},{1,97},{128,160},{129,225},{8,40},{9,105},{136,168},{137,23... | collective-permute-start | bytes 2359304 | tf_op jit(solution)/shard_map/ppermute | solution.py:31
  67.7 0.0 collective-permute-start.18
  67.7 2.9 %collective-permute-done.14.refs_11_ = bf16[4,1024,128]{2,1,0:T(8,128)(2,1)S(1)} collective-permute-done((bf16[4,1024,128]{2,1,0:T(8,128)(2,1)S(1)}, bf16[4,1024,128]{2,1,0:T(8,128)(2,1)S(1)}, u32[]{:S(2)}, u32[]{:S(2)}) %collective-permute-start.14) | collective-permute-done | bytes 1048608 | tf_op jit(solution)/shard_map/ppermute | solution.py:31
  70.6 0.6 broadcast_add_fusion.table
  71.1 0.0 collective-permute-done.15.refs_12_
  71.1 0.4 copy-done.12
  71.5 1.4 %copy-done.8 = bf16[9,1024,128]{2,1,0:T(8,128)(2,1)} copy-done((bf16[9,1024,128]{2,1,0:T(8,128)(2,1)}, bf16[9,1024,128]{2,1,0:T(8,128)(2,1)S(1)}, u32[]{:S(2)}) %copy-start.8) | copy-done | bytes 2359320
  72.9 11.4 %shard_map.56 = (f32[1024,768]{1,0:T(8,128)}, bf16[12,1024,128]{2,1,0:T(8,128)(2,1)}) custom-call(s32[40]{0:T(128)} %broadcast_add_fusion.table, f32[1024,768]{1,0:T(8,128)} %hessian.1, bf16[1,1024,128]{2,1,0:T(8,128)(2,1)} %shard_map.55.refs_0_, bf16[1,1024,128]{2,1,0:T(8,128)(2,1)} %copy-done, bf16[1,1024,128]{2,1,0:T(8,128)(2,1)} %copy-done.9, ...), custom_call_target="tpu_custom_call" | custom-call | flops 4026531840 | bytes 15466496 | tf_op jit(solution)/shard_map/pallas_call | solution.py:278
  84.4 0.0 collective-permute-done.17.refs_1_
  84.4 0.0 copy-start.18
  84.4 1.2 %collective-permute-done.16.refs_0_ = bf16[512,768]{1,0:T(8,128)(2,1)} collective-permute-done((bf16[512,768]{1,0:T(8,128)(2,1)S(1)}, bf16[512,768]{1,0:T(8,128)(2,1)}, u32[]{:S(2)}, u32[]{:S(2)}) %collective-permute-start.16) | collective-permute-done | bytes 786464 | tf_op jit(solution)/shard_map/ppermute | solution.py:31
  85.5 0.8 collective-permute-done.18.refs_2_
  86.3 5.7 %shard_map.57 = f32[1024,768]{1,0:T(8,128)} custom-call(f32[1024,768]{1,0:T(8,128)} %get-tuple-element.148.partial, bf16[12,1024,128]{2,1,0:T(8,128)(2,1)} %get-tuple-element.149.late_rows, bf16[512,768]{1,0:T(8,128)(2,1)} %collective-permute-done.16.refs_0_, bf16[512,768]{1,0:T(8,128)(2,1)} %copy-done.18, bf16[512,768]{1,0:T(8,128)(2,1)} %collective-permute-done.18.refs_2_), custom_call_target="tpu_custom_call" | custom-call | flops 2415919104 | bytes 11796480 | tf_op jit(solution)/shard_map/pallas_call | solution.py:298
  (39 shorter events, 0.1 us)
Async XLA Ops:
  2.1 16.9 %collective-permute-start = (bf16[1,1024,128]{2,1,0:T(8,128)(2,1)}, bf16[1,1024,128]{2,1,0:T(8,128)(2,1)S(1)}, u32[]{:S(2)}, u32[]{:S(2)}) collective-permute-start(bf16[1,1024,128]{2,1,0:T(8,128)(2,1)} %shard_map.55.refs_0_), channel_id=1, source_target_pairs={{0,8},{1,25},{128,136},{129,153},{8,16},{9,1},{136,144},{137,129},... | collective-permute-start | bytes 786440 | tf_op jit(solution)/shard_map/ppermute | solution.py:31
  9.0 10.0 %collective-permute-start.1 = (bf16[1,1024,128]{2,1,0:T(8,128)(2,1)}, bf16[1,1024,128]{2,1,0:T(8,128)(2,1)S(1)}, u32[]{:S(2)}, u32[]{:S(2)}) collective-permute-start(bf16[1,1024,128]{2,1,0:T(8,128)(2,1)} %shard_map.55.refs_0_), channel_id=1, source_target_pairs={{0,2},{1,7},{128,130},{129,135},{8,10},{9,15},{136,138},{137,143},... | collective-permute-start | bytes 786440 | tf_op jit(solution)/shard_map/ppermute | solution.py:31
  11.7 7.3 %collective-permute-start.2 = (bf16[1,1024,128]{2,1,0:T(8,128)(2,1)}, bf16[1,1024,128]{2,1,0:T(8,128)(2,1)S(1)}, u32[]{:S(2)}, u32[]{:S(2)}) collective-permute-start(bf16[1,1024,128]{2,1,0:T(8,128)(2,1)} %shard_map.55.refs_0_), channel_id=1, source_target_pairs={{0,6},{1,3},{128,134},{129,131},{8,14},{9,11},{136,142},{137,139},... | collective-permute-start | bytes 786440 | tf_op jit(solution)/shard_map/ppermute | solution.py:31
  11.7 11.8 %collective-permute-start.3 = (bf16[1,1024,128]{2,1,0:T(8,128)(2,1)}, bf16[1,1024,128]{2,1,0:T(8,128)(2,1)S(1)}, u32[]{:S(2)}, u32[]{:S(2)}) collective-permute-start(bf16[1,1024,128]{2,1,0:T(8,128)(2,1)} %shard_map.55.refs_0_), channel_id=1, source_target_pairs={{0,24},{1,9},{128,152},{129,137},{8,0},{9,17},{136,128},{137,145},... | collective-permute-start | bytes 786440 | tf_op jit(solution)/shard_map/ppermute | solution.py:31
  13.6 16.9 %copy-start.6 = (bf16[512,768]{1,0:T(8,128)(2,1)}, bf16[512,768]{1,0:T(8,128)(2,1)S(1)}, u32[]{:S(2)}) copy-start(bf16[512,768]{1,0:T(8,128)(2,1)S(1)} %fusion.4.refs_13_) | copy-start | bytes 2359300
  13.6 15.1 %collective-permute-start.4 = (bf16[512,768]{1,0:T(8,128)(2,1)S(1)}, bf16[512,768]{1,0:T(8,128)(2,1)S(1)}, u32[]{:S(2)}, u32[]{:S(2)}) collective-permute-start(bf16[512,768]{1,0:T(8,128)(2,1)S(1)} %fusion.4.refs_13_), channel_id=1, source_target_pairs={{0,96},{1,33},{128,224},{129,161},{8,104},{9,41},{136,232},{137,16... | collective-permute-start | bytes 2359304 | tf_op jit(solution)/shard_map/ppermute | solution.py:31
  19.0 11.5 %copy-start = (bf16[1,1024,128]{2,1,0:T(8,128)(2,1)}, bf16[1,1024,128]{2,1,0:T(8,128)(2,1)S(1)}, u32[]{:S(2)}) copy-start(bf16[1,1024,128]{2,1,0:T(8,128)(2,1)S(1)} %collective-permute-done.refs_1_) | copy-start | bytes 786436
  19.0 11.5 %copy-start.9 = (bf16[1,1024,128]{2,1,0:T(8,128)(2,1)}, bf16[1,1024,128]{2,1,0:T(8,128)(2,1)S(1)}, u32[]{:S(2)}) copy-start(bf16[1,1024,128]{2,1,0:T(8,128)(2,1)S(1)} %collective-permute-done.1.refs_2_) | copy-start | bytes 786436
  19.1 11.5 %copy-start.10 = (bf16[1,1024,128]{2,1,0:T(8,128)(2,1)}, bf16[1,1024,128]{2,1,0:T(8,128)(2,1)S(1)}, u32[]{:S(2)}) copy-start(bf16[1,1024,128]{2,1,0:T(8,128)(2,1)S(1)} %collective-permute-done.2.refs_3_) | copy-start | bytes 786436
  19.1 9.5 %collective-permute-start.5 = (bf16[1,1024,128]{2,1,0:T(8,128)(2,1)S(1)}, bf16[1,1024,128]{2,1,0:T(8,128)(2,1)S(1)}, u32[]{:S(2)}, u32[]{:S(2)}) collective-permute-start(bf16[1,1024,128]{2,1,0:T(8,128)(2,1)S(1)} %collective-permute-done.refs_1_), channel_id=1, source_target_pairs={{0,8},{1,25},{128,136},{129,153},{8,16},{9,1},{136,144},{137,129},... | collective-permute-start | bytes 786440 | tf_op jit(solution)/shard_map/ppermute | solution.py:31
  23.5 7.0 %copy-start.1 = (bf16[1,1024,128]{2,1,0:T(8,128)(2,1)}, bf16[1,1024,128]{2,1,0:T(8,128)(2,1)S(1)}, u32[]{:S(2)}) copy-start(bf16[1,1024,128]{2,1,0:T(8,128)(2,1)S(1)} %collective-permute-done.3.refs_4_) | copy-start | bytes 786436
  23.5 5.9 %collective-permute-start.6 = (bf16[1,1024,128]{2,1,0:T(8,128)(2,1)S(1)}, bf16[1,1024,128]{2,1,0:T(8,128)(2,1)S(1)}, u32[]{:S(2)}, u32[]{:S(2)}) collective-permute-start(bf16[1,1024,128]{2,1,0:T(8,128)(2,1)S(1)} %collective-permute-done.1.refs_2_), channel_id=1, source_target_pairs={{0,2},{1,7},{128,130},{129,135},{8,10},{9,15},{136,138},{137,143},... | collective-permute-start | bytes 786440 | tf_op jit(solution)/shard_map/ppermute | solution.py:31
  26.1 11.4 %collective-permute-start.7 = (bf16[512,768]{1,0:T(8,128)(2,1)S(1)}, bf16[512,768]{1,0:T(8,128)(2,1)S(1)}, u32[]{:S(2)}, u32[]{:S(2)}) collective-permute-start(bf16[512,768]{1,0:T(8,128)(2,1)S(1)} %fusion.4.refs_13_), channel_id=1, source_target_pairs={{0,32},{1,97},{128,160},{129,225},{8,40},{9,105},{136,168},{137,23... | collective-permute-start | bytes 2359304 | tf_op jit(solution)/shard_map/ppermute | solution.py:31
  28.6 18.5 %collective-permute-start.8 = (bf16[512,768]{1,0:T(8,128)(2,1)S(1)}, bf16[512,768]{1,0:T(8,128)(2,1)S(1)}, u32[]{:S(2)}, u32[]{:S(2)}) collective-permute-start(bf16[512,768]{1,0:T(8,128)(2,1)S(1)} %fusion.4.refs_13_), channel_id=1, source_target_pairs={{0,128},{1,129},{128,0},{129,1},{8,136},{9,137},{136,8},{137,9},{1... | collective-permute-start | bytes 2359304 | tf_op jit(solution)/shard_map/ppermute | solution.py:31
  28.6 2.0 %copy-start.7 = (bf16[1,1024,128]{2,1,0:T(8,128)(2,1)S(1)}, bf16[1,1024,128]{2,1,0:T(8,128)(2,1)}, u32[]{:S(2)}) copy-start(bf16[1,1024,128]{2,1,0:T(8,128)(2,1)} %shard_map.55.refs_0_) | copy-start | bytes 786436
  28.6 2.0 %copy-start.2 = (bf16[1,1024,128]{2,1,0:T(8,128)(2,1)}, bf16[1,1024,128]{2,1,0:T(8,128)(2,1)S(1)}, u32[]{:S(2)}) copy-start(bf16[1,1024,128]{2,1,0:T(8,128)(2,1)S(1)} %collective-permute-done.5.refs_5_) | copy-start | bytes 786436
  28.7 2.0 %copy-start.13 = (bf16[512,768]{1,0:T(8,128)(2,1)}, bf16[512,768]{1,0:T(8,128)(2,1)S(1)}, u32[]{:S(2)}) copy-start(bf16[512,768]{1,0:T(8,128)(2,1)S(1)} %collective-permute-done.4.refs_16_) | copy-start | bytes 2359300
  28.8 18.2 %collective-permute-start.9 = (bf16[3,1024,128]{2,1,0:T(8,128)(2,1)S(1)}, bf16[3,1024,128]{2,1,0:T(8,128)(2,1)S(1)}, u32[]{:S(2)}, u32[]{:S(2)}) collective-permute-start(bf16[3,1024,128]{2,1,0:T(8,128)(2,1)S(1)} %pad_maximum_fusion.2), channel_id=1, source_target_pairs={{0,2},{1,7},{128,130},{129,135},{8,10},{9,15},{136,138},{137,143},... | collective-permute-start | bytes 2359304 | tf_op jit(solution)/shard_map/ppermute | solution.py:31
  29.4 29.5 %copy-start.11 = (bf16[1,1024,128]{2,1,0:T(8,128)(2,1)}, bf16[1,1024,128]{2,1,0:T(8,128)(2,1)S(1)}, u32[]{:S(2)}) copy-start(bf16[1,1024,128]{2,1,0:T(8,128)(2,1)S(1)} %collective-permute-done.6.refs_6_) | copy-start | bytes 786436
  29.4 20.2 %collective-permute-start.10 = (bf16[3,1024,128]{2,1,0:T(8,128)(2,1)S(1)}, bf16[3,1024,128]{2,1,0:T(8,128)(2,1)S(1)}, u32[]{:S(2)}, u32[]{:S(2)}) collective-permute-start(bf16[3,1024,128]{2,1,0:T(8,128)(2,1)S(1)} %pad_maximum_fusion.4), channel_id=1, source_target_pairs={{0,6},{1,3},{128,134},{129,131},{8,14},{9,11},{136,142},{137,139},... | collective-permute-start | bytes 2359304 | tf_op jit(solution)/shard_map/ppermute | solution.py:31
  37.5 21.5 %copy-start.15 = (bf16[512,768]{1,0:T(8,128)(2,1)}, bf16[512,768]{1,0:T(8,128)(2,1)S(1)}, u32[]{:S(2)}) copy-start(bf16[512,768]{1,0:T(8,128)(2,1)S(1)} %collective-permute-done.7.refs_15_) | copy-start | bytes 2359300
  37.5 12.3 %collective-permute-start.11 = (bf16[512,768]{1,0:T(8,128)(2,1)S(1)}, bf16[512,768]{1,0:T(8,128)(2,1)S(1)}, u32[]{:S(2)}, u32[]{:S(2)}) collective-permute-start(bf16[512,768]{1,0:T(8,128)(2,1)S(1)} %collective-permute-done.7.refs_15_), channel_id=1, source_target_pairs={{0,32},{1,97},{128,160},{129,225},{8,40},{9,105},{136,168},{137,23... | collective-permute-start | bytes 2359304 | tf_op jit(solution)/shard_map/ppermute | solution.py:31
  47.0 19.2 %copy-start.14 = (bf16[512,768]{1,0:T(8,128)(2,1)}, bf16[512,768]{1,0:T(8,128)(2,1)S(1)}, u32[]{:S(2)}) copy-start(bf16[512,768]{1,0:T(8,128)(2,1)S(1)} %collective-permute-done.8.refs_14_) | copy-start | bytes 2359300
  47.0 2.8 %collective-permute-start.12 = (bf16[3,1024,128]{2,1,0:T(8,128)(2,1)S(1)}, bf16[3,1024,128]{2,1,0:T(8,128)(2,1)S(1)}, u32[]{:S(2)}, u32[]{:S(2)}) collective-permute-start(bf16[3,1024,128]{2,1,0:T(8,128)(2,1)S(1)} %pad_maximum_fusion.5), channel_id=1, source_target_pairs={{0,1},{1,0},{128,129},{129,128},{8,9},{9,8},{136,137},{137,136},{1... | collective-permute-start | bytes 2359304 | tf_op jit(solution)/shard_map/ppermute | solution.py:31
  47.0 11.9 %copy-start.3 = (bf16[3,1024,128]{2,1,0:T(8,128)(2,1)}, bf16[3,1024,128]{2,1,0:T(8,128)(2,1)S(1)}, u32[]{:S(2)}) copy-start(bf16[3,1024,128]{2,1,0:T(8,128)(2,1)S(1)} %collective-permute-done.9.refs_7_) | copy-start | bytes 2359300
  47.1 11.6 %collective-permute-start.13 = (bf16[3,1024,128]{2,1,0:T(8,128)(2,1)S(1)}, bf16[3,1024,128]{2,1,0:T(8,128)(2,1)S(1)}, u32[]{:S(2)}, u32[]{:S(2)}) collective-permute-start(bf16[3,1024,128]{2,1,0:T(8,128)(2,1)S(1)} %collective-permute-done.9.refs_7_), channel_id=1, source_target_pairs={{0,2},{1,7},{128,130},{129,135},{8,10},{9,15},{136,138},{137,143},... | collective-permute-start | bytes 2359304 | tf_op jit(solution)/shard_map/ppermute | solution.py:31
  49.6 9.4 %copy-start.4 = (bf16[3,1024,128]{2,1,0:T(8,128)(2,1)}, bf16[3,1024,128]{2,1,0:T(8,128)(2,1)S(1)}, u32[]{:S(2)}) copy-start(bf16[3,1024,128]{2,1,0:T(8,128)(2,1)S(1)} %collective-permute-done.10.refs_8_) | copy-start | bytes 2359300
  49.8 17.8 %copy-start.16 = (bf16[512,768]{1,0:T(8,128)(2,1)}, bf16[512,768]{1,0:T(8,128)(2,1)S(1)}, u32[]{:S(2)}) copy-start(bf16[512,768]{1,0:T(8,128)(2,1)S(1)} %collective-permute-done.11.refs_17_) | copy-start | bytes 2359300
  49.9 0.9 copy-start.17
  58.7 9.0 %copy-start.5 = (bf16[3,1024,128]{2,1,0:T(8,128)(2,1)}, bf16[3,1024,128]{2,1,0:T(8,128)(2,1)S(1)}, u32[]{:S(2)}) copy-start(bf16[3,1024,128]{2,1,0:T(8,128)(2,1)S(1)} %collective-permute-done.13.refs_10_) | copy-start | bytes 2359300
  59.0 12.2 %collective-permute-start.15 = (bf16[9,1024,128]{2,1,0:T(8,128)(2,1)S(1)}, bf16[9,1024,128]{2,1,0:T(8,128)(2,1)S(1)}, u32[]{:S(2)}, u32[]{:S(2)}) collective-permute-start(bf16[9,1024,128]{2,1,0:T(8,128)(2,1)S(1)} %pad_maximum_fusion), channel_id=1, source_target_pairs={{0,1},{1,0},{128,129},{129,128},{8,9},{9,8},{136,137},{137,136},{1... | collective-permute-start | bytes 7077896 | tf_op jit(solution)/shard_map/ppermute | solution.py:31
  64.9 5.7 %collective-permute-start.14 = (bf16[4,1024,128]{2,1,0:T(8,128)(2,1)S(1)}, bf16[4,1024,128]{2,1,0:T(8,128)(2,1)S(1)}, u32[]{:S(2)}, u32[]{:S(2)}) collective-permute-start(bf16[4,1024,128]{2,1,0:T(8,128)(2,1)S(1)} %pad_maximum_fusion.1), channel_id=1, source_target_pairs={{0,1},{1,0},{128,129},{129,128},{8,9},{9,8},{136,137},{137,136},{1... | collective-permute-start | bytes 3145736 | tf_op jit(solution)/shard_map/ppermute | solution.py:31
  65.0 19.4 %collective-permute-start.17 = (bf16[512,768]{1,0:T(8,128)(2,1)S(1)}, bf16[512,768]{1,0:T(8,128)(2,1)S(1)}, u32[]{:S(2)}, u32[]{:S(2)}) collective-permute-start(bf16[512,768]{1,0:T(8,128)(2,1)S(1)} %collective-permute-done.8.refs_14_), channel_id=1, source_target_pairs={{0,96},{1,33},{128,224},{129,161},{8,104},{9,41},{136,232},{137,16... | collective-permute-start | bytes 2359304 | tf_op jit(solution)/shard_map/ppermute | solution.py:31
  66.2 19.3 %collective-permute-start.16 = (bf16[512,768]{1,0:T(8,128)(2,1)S(1)}, bf16[512,768]{1,0:T(8,128)(2,1)}, u32[]{:S(2)}, u32[]{:S(2)}) collective-permute-start(bf16[512,768]{1,0:T(8,128)(2,1)S(1)} %collective-permute-done.8.refs_14_), channel_id=1, source_target_pairs={{0,32},{1,97},{128,160},{129,225},{8,40},{9,105},{136,168},{137,23... | collective-permute-start | bytes 2359304 | tf_op jit(solution)/shard_map/ppermute | solution.py:31
  67.7 18.6 %collective-permute-start.18 = (bf16[512,768]{1,0:T(8,128)(2,1)S(1)}, bf16[512,768]{1,0:T(8,128)(2,1)}, u32[]{:S(2)}, u32[]{:S(2)}) collective-permute-start(bf16[512,768]{1,0:T(8,128)(2,1)S(1)} %collective-permute-done.11.refs_17_), channel_id=1, source_target_pairs={{0,128},{1,129},{128,0},{129,1},{8,136},{9,137},{136,8},{137,9},{1... | collective-permute-start | bytes 2359304 | tf_op jit(solution)/shard_map/ppermute | solution.py:31
  70.6 1.0 %copy-start.12 = (bf16[4,1024,128]{2,1,0:T(8,128)(2,1)}, bf16[4,1024,128]{2,1,0:T(8,128)(2,1)S(1)}, u32[]{:S(2)}) copy-start(bf16[4,1024,128]{2,1,0:T(8,128)(2,1)S(1)} %collective-permute-done.14.refs_11_) | copy-start | bytes 3145732
  71.5 1.4 %copy-start.8 = (bf16[9,1024,128]{2,1,0:T(8,128)(2,1)}, bf16[9,1024,128]{2,1,0:T(8,128)(2,1)S(1)}, u32[]{:S(2)}) copy-start(bf16[9,1024,128]{2,1,0:T(8,128)(2,1)S(1)} %collective-permute-done.15.refs_12_) | copy-start | bytes 7077892
  84.4 1.9 %copy-start.18 = (bf16[512,768]{1,0:T(8,128)(2,1)}, bf16[512,768]{1,0:T(8,128)(2,1)S(1)}, u32[]{:S(2)}) copy-start(bf16[512,768]{1,0:T(8,128)(2,1)S(1)} %collective-permute-done.17.refs_1_) | copy-start | bytes 2359300
